TPU v7x, 256 devices: a whole 4x4x8 slice. The times are simulated.
256 devices in a mesh: rep: 16 (over y, z_lo, core), fsdp: 16 (over z_hi, x).
Axes of the slice: x: 4, y: 4, z: 8 (z_hi: 4, z_lo: 2; z = z_hi * 2 + z_lo), core: 2. Of those that a mesh axis runs over, the one named last changes fastest.
Arguments:
- tokens: bfloat16 [65536, 6144], P(('rep', 'fsdp')), may hold values from -6 to 6
- targets: bfloat16 [65536, 1024], P(('rep', 'fsdp')), may hold values from -6 to 6
- weight: bfloat16 [16, 6144, 1024], P('rep', 'fsdp'), may hold values from -6 to 6
- moment_first: float32 [16, 6144, 1024], P('rep', 'fsdp'), may hold values from -6 to 6
- moment_second: float32 [16, 6144, 1024], P('rep', 'fsdp'), may hold values from 0.5 to 4
- fragment_local: bfloat16 [16, 6144, 1024], P('rep', 'fsdp'), may hold values from -6 to 6
- global_params: float32 [2, 6144, 1024], P(None, 'fsdp', 'rep'), may hold values from -6 to 6
- outer_moment: float32 [2, 6144, 1024], P(None, 'fsdp', 'rep'), may hold values from -4 to 4
- fragment: int32 [1], replicated, may hold values from 0 to 1
Outputs:
- new_weight: bfloat16 [16, 6144, 1024], P('rep', 'fsdp')
- new_first: float32 [16, 6144, 1024], P('rep', 'fsdp')
- new_second: float32 [16, 6144, 1024], P('rep', 'fsdp')
- new_fragment: bfloat16 [16, 6144, 1024], P('rep', 'fsdp')
- new_global: float32 [2, 6144, 1024], P(None, 'fsdp', 'rep')
- new_outer: float32 [2, 6144, 1024], P(None, 'fsdp', 'rep')
All inputs are finite; a program needn't handle non-finite values.
Results may differ from a plain program's by a relative error of at most 0.013.
Values may be sent and summed in bfloat16 or wider, within the bound.
No kernel may reach another device: no remote copies, remote signals or barrier semaphores. Data moves between devices by JAX's collectives and lax.ppermute only.
A program may use at most 128 MiB of HBM per device.

v0:
```python
import math

import jax
import jax.numpy as jnp
from jax import lax
from jax.experimental import pallas as pl
from jax.experimental.pallas import tpu as pltpu
from jax.sharding import PartitionSpec as P

CHUNKS = 2
NX = 4
NZ = 4
NY = 4
LIMIT = 16 * 2**20
LIGHT = pl.CostEstimate(flops=1, bytes_accessed=1, transcendentals=0)
HEAVY = pl.CostEstimate(flops=4 * 10**10, bytes_accessed=10**6, transcendentals=0)

f32 = jnp.float32
bf16 = jnp.bfloat16


def along_x(value, step):
    pairs = [(a * NX + b, a * NX + (b + step) % NX) for a in range(NZ) for b in range(NX)]
    return lax.ppermute(value, "fsdp", pairs)


def along_z(value, step):
    pairs = [(a * NX + b, (a + step) % NZ * NX + b) for a in range(NZ) for b in range(NX)]
    return lax.ppermute(value, "fsdp", pairs)


def swap_near(value):
    return lax.ppermute(value, "rep", [(r, r ^ 4) for r in range(16)])


def swap_far(value):
    return lax.ppermute(value, "rep", [(r, r ^ 8) for r in range(16)])


def swap_core(value):
    return lax.ppermute(value, "rep", [(r, r ^ 1) for r in range(16)])


def swap_pair(value):
    return lax.ppermute(value, "rep", [(r, r ^ 2) for r in range(16)])


def kernel_call(kernel, inputs, outs, cost, name, scratch=(), blocked=None, **options):
    blocked = blocked or {}
    specs = [
        blocked.get(n, pl.BlockSpec(memory_space=pltpu.VMEM)) for n in range(len(inputs))
    ]
    inputs = [
        value if n in blocked else pltpu.with_memory_space_constraint(value, pltpu.VMEM)
        for n, value in enumerate(inputs)
    ]
    return pl.pallas_call(
        kernel,
        in_specs=specs,
        out_specs=[pl.BlockSpec(memory_space=pltpu.VMEM)] * len(outs),
        out_shape=[pltpu.VMEM(shape, dtype) for shape, dtype in outs],
        scratch_shapes=list(scratch),
        compiler_params=pltpu.CompilerParams(vmem_limit_bytes=LIMIT),
        cost_estimate=cost,
        name=name,
        **options,
    )(*inputs)


SMALL = pl.BlockSpec(memory_space=pltpu.SMEM)
ANYWHERE = pl.BlockSpec(memory_space=pl.ANY)
IN_HBM = pl.BlockSpec(memory_space=pltpu.HBM)


def in_hbm(value):
    return pltpu.with_memory_space_constraint(value, pltpu.HBM)


def pack_tokens(tokens):
    rows, width = tokens.shape
    block = width // (NX * NZ)
    me = lax.axis_index("fsdp").astype(jnp.int32).reshape(1)

    def kernel(me_ref, source, *refs):
        sems = refs[-1]
        z, x = me_ref[0] // NX, me_ref[0] % NX
        copies = []
        for k in range(NX):
            for j in range(NZ):
                start = ((z + j) % NZ * NX + (x + k) % NX) * block
                copies.append(
                    pltpu.make_async_copy(
                        source.at[:, pl.ds(pl.multiple_of(start, 128), block)],
                        refs[k].at[:, j * block : (j + 1) * block],
                        sems.at[k, j],
                    )
                )
        for copy in copies:
            copy.start()
        for copy in copies:
            copy.wait()

    return kernel_call(
        kernel,
        [me, tokens],
        [((rows, NZ * block), tokens.dtype)] * NX,
        LIGHT,
        "pack_tokens",
        scratch=[pltpu.SemaphoreType.DMA((NX, NZ))],
        blocked={0: SMALL, 1: ANYWHERE},
    )


def load(arrays, name):
    count = len(arrays)

    def kernel(*refs):
        copies = [
            pltpu.make_async_copy(refs[n], refs[count + n], refs[-1].at[n]) for n in range(count)
        ]
        for copy in copies:
            copy.start()
        for copy in copies:
            copy.wait()

    return kernel_call(
        kernel,
        [in_hbm(array) for array in arrays],
        [(array.shape, array.dtype) for array in arrays],
        LIGHT,
        name,
        scratch=[pltpu.SemaphoreType.DMA((count,))],
        blocked={n: IN_HBM for n in range(count)},
    )


def transpose_tokens(pieces):
    rows, width = pieces[0].shape

    def kernel(*refs):
        out = refs[-1]
        for k in range(NX):
            out[:, k * rows : (k + 1) * rows] = refs[k][...].T

    return kernel_call(
        kernel, pieces, [((width, NX * rows), bf16)], HEAVY, "transpose_tokens"
    )[0]


def split_columns(value, parts):
    rows, width = value.shape
    columns = width // parts

    def kernel(source, *refs):
        copies = [
            pltpu.make_async_copy(
                source.at[:, c * columns : (c + 1) * columns], refs[c], refs[-1].at[c]
            )
            for c in range(parts)
        ]
        for copy in copies:
            copy.start()
        for copy in copies:
            copy.wait()

    return kernel_call(
        kernel,
        [value],
        [((rows, columns), value.dtype)] * parts,
        LIGHT,
        "split_columns",
        scratch=[pltpu.SemaphoreType.DMA((parts,))],
        blocked={0: ANYWHERE},
    )


def outer_halves(previous, following):
    half = previous.shape[0] // 2

    def kernel(previous, following, top, bottom):
        top[...] = previous[:half, :]
        bottom[...] = following[half:, :]

    return kernel_call(
        kernel, [previous, following], [((half, previous.shape[1]), bf16)] * 2, LIGHT, "outer_halves"
    )


def partial_keys(pieces, blocks, cost):
    rows, width = pieces[0].shape
    columns = blocks[0].shape[1]

    def kernel(*refs):
        tokens = refs[:NX]
        weights = refs[NX : NX + len(blocks)]
        outs = refs[NX + len(blocks) : -1]
        whole = refs[-1]
        at = 0
        for ref in weights:
            whole[at : at + ref.shape[0], :] = ref[...]
            at += ref.shape[0]
        for k in (2, 1, 3, 0):
            outs[k][...] = jnp.dot(
                tokens[k][...], whole[...], preferred_element_type=f32
            ).astype(outs[k].dtype)

    return kernel_call(
        kernel,
        [*pieces, *blocks],
        [((rows, columns), f32 if k == 0 else bf16) for k in range(NX)],
        cost,
        "partial_keys",
        scratch=[pltpu.VMEM((width, columns), bf16)],
    )


def residual(own, others, goals, part, inv_root):
    chosen = slice(part * own.shape[1], (part + 1) * own.shape[1])

    def kernel(own, one, two, three, goals, out):
        total = own[...] + one[...].astype(f32) + two[...].astype(f32) + three[...].astype(f32)
        out[...] = (total * inv_root - goals[:, chosen].astype(f32)).astype(bf16)

    return kernel_call(kernel, [own, *others, goals], [(own.shape, bf16)], LIGHT, "residual")[0]


def partial_grad(turned, resids):
    width, tokens = turned.shape
    rows, columns = resids[0].shape
    block = width // NZ
    half = block // 2

    def kernel(turned_ref, *refs):
        resid = refs[:NX]
        own, one, far_a, far_b, three, whole = refs[NX:]
        for k in range(NX):
            whole[k * rows : (k + 1) * rows, :] = resid[k][...]
        far = jnp.dot(
            turned_ref[2 * block : 3 * block, :], whole[...], preferred_element_type=f32
        )
        far_a[...] = far[:half].astype(bf16)
        far_b[...] = far[half:].astype(bf16)
        for j, out in ((1, one), (3, three), (0, own)):
            out[...] = jnp.dot(
                turned_ref[j * block : (j + 1) * block, :], whole[...], preferred_element_type=f32
            ).astype(out.dtype)

    return kernel_call(
        kernel,
        [turned, *resids],
        [
            ((block, columns), f32),
            ((block, columns), bf16),
            ((half, columns), bf16),
            ((half, columns), bf16),
            ((block, columns), bf16),
        ],
        HEAVY,
        "partial_grad",
        scratch=[pltpu.VMEM((tokens, columns), bf16)],
    )


def add_halves(one, far_a, three, far_b):
    half = far_a.shape[0]

    def kernel(one, far_a, three, far_b, up, down):
        up[:half, :] = (one[:half, :].astype(f32) + far_a[...].astype(f32)).astype(bf16)
        up[half:, :] = one[half:, :]
        down[:half, :] = three[:half, :]
        down[half:, :] = (three[half:, :].astype(f32) + far_b[...].astype(f32)).astype(bf16)

    return kernel_call(
        kernel, [one, far_a, three, far_b], [(one.shape, bf16)] * 2, LIGHT, "add_halves"
    )


def adam_columns(part, parts, scale, own, left, right, weight, first, second, earlier):
    rows, width = weight.shape
    columns = width // parts
    tiles = 3
    tile = rows // tiles
    chosen = slice(part * columns, (part + 1) * columns)

    def kernel(own, left, right, weight, first, second, *refs):
        new_weight, new_first, new_second = refs[-3:]
        at = pl.ds(pl.multiple_of(pl.program_id(0) * tile, tile), tile)
        grad = (own[at, :] + left[at, :].astype(f32) + right[at, :].astype(f32)) * scale
        moved = 0.9 * first[at, chosen] + 0.1 * grad
        spread = 0.95 * second[at, chosen] + 0.05 * grad * grad
        wide = weight[at, chosen].astype(f32)
        new_first[...] = moved
        new_second[...] = spread
        new_weight[...] = (wide - 0.3 * (moved / (jnp.sqrt(spread) + 1e-08) + 0.1 * wide)).astype(
            bf16
        )

    inputs = [own, left, right, weight, first, second]
    place = pl.BlockSpec((tile, columns), lambda i: (i, part))
    return pl.pallas_call(
        kernel,
        grid=(tiles,),
        in_specs=[pl.BlockSpec(memory_space=pltpu.VMEM)] * 6
        + [ANYWHERE] * (3 if earlier else 0),
        out_specs=[place] * 3,
        out_shape=[
            jax.ShapeDtypeStruct((rows, width), bf16),
            jax.ShapeDtypeStruct((rows, width), f32),
            jax.ShapeDtypeStruct((rows, width), f32),
        ],
        input_output_aliases={6 + n: n for n in range(3)} if earlier else {},
        compiler_params=pltpu.CompilerParams(vmem_limit_bytes=LIMIT),
        cost_estimate=LIGHT,
        name="adam_columns",
    )(*[pltpu.with_memory_space_constraint(value, pltpu.VMEM) for value in inputs], *(earlier or ()))


def turn_fragment(fragment, core):
    rows, width = fragment.shape
    columns = width // 16

    def kernel(core_ref, source, mine, other):
        low = core_ref[0] == 0
        for y in range(NY):
            for pair in range(2):
                at = (y * 2 + pair) * 2 * columns
                both = source[:, at : at + 2 * columns].T
                mine[y, pair] = jnp.where(low, both[:columns], both[columns:])
                other[y, pair] = jnp.where(low, both[columns:], both[:columns])

    return kernel_call(
        kernel,
        [core, fragment],
        [((NY, 2, columns, rows), bf16)] * 2,
        LIGHT,
        "turn_fragment",
        blocked={0: SMALL},
    )


def halve(mine, other, keep, name):
    shape = (mine.shape[0] // 2, *mine.shape[1:])

    def kernel(keep_ref, mine, other, kept, sent):
        for out, which in ((sent, 1 - keep_ref[0]), (kept, keep_ref[0])):
            at = pl.ds(which * shape[0], shape[0])
            out[...] = mine[at].astype(f32) + other[at].astype(f32)

    return kernel_call(
        kernel,
        [keep, mine, other],
        [(shape, f32)] * 2,
        LIGHT,
        name,
        blocked={0: SMALL},
    )


def total(mine, other):
    def kernel(mine, other, out):
        out[...] = mine[...] + other[...]

    return kernel_call(kernel, [mine, other], [(mine.shape, f32)], LIGHT, "total")[0]


def stack(mine, other, second, name):
    count = mine.shape[0]

    def kernel(second_ref, mine, other, out):
        out[pl.ds(second_ref[0] * count, count)] = mine[...]
        out[pl.ds((1 - second_ref[0]) * count, count)] = other[...]

    return kernel_call(
        kernel,
        [second, mine, other],
        [((2 * count, *mine.shape[1:]), mine.dtype)],
        LIGHT,
        name,
        blocked={0: SMALL},
    )[0]


def chosen_params(globs, outers, index):
    def kernel(index_ref, globs, outers, out):
        out[0] = globs[index_ref[0]]
        out[1] = outers[index_ref[0]]

    return kernel_call(
        kernel,
        [index, globs, outers],
        [((2, *globs.shape[1:]), f32)],
        LIGHT,
        "chosen_params",
        blocked={0: SMALL},
    )[0]


def nesterov(mine, other, own, theirs, globs, outers, index, pair, replicas):
    frags = globs.shape[0]

    def kernel(index_ref, pair_ref, mine, other, own, theirs, globs, outers, *outs):
        updated, new_global, new_outer = outs
        new_global[...] = globs[...]
        new_outer[...] = outers[...]
        for which, params in ((pair_ref[0], own), (1 - pair_ref[0], theirs)):
            mean_local = (mine[which] + other[which]) / replicas
            glob = params[0]
            moment = 0.9 * params[1] + (glob - mean_local)
            after = glob - 0.7 * (glob - mean_local + 0.9 * moment)
            updated[which] = after.astype(bf16)
            if params is own:
                new_global[index_ref[0]] = after
                new_outer[index_ref[0]] = moment

    return pl.pallas_call(
        kernel,
        in_specs=[SMALL] * 2 + [pl.BlockSpec(memory_space=pltpu.VMEM)] * 6,
        out_specs=[pl.BlockSpec(memory_space=pltpu.VMEM)] + [pl.BlockSpec()] * 2,
        out_shape=[
            pltpu.VMEM(mine.shape, bf16),
            jax.ShapeDtypeStruct(globs.shape, f32),
            jax.ShapeDtypeStruct(globs.shape, f32),
        ],
        compiler_params=pltpu.CompilerParams(vmem_limit_bytes=LIMIT),
        cost_estimate=LIGHT,
        name="nesterov",
    )(
        index,
        pair,
        *[
            pltpu.with_memory_space_constraint(value, pltpu.VMEM)
            for value in (mine, other, own, theirs, globs, outers)
        ],
    )


def weave(mine, other, core):
    ys, pairs, columns, rows = mine.shape

    def kernel(core_ref, mine, other, out):
        low = core_ref[0] == 0
        for y in range(ys):
            for pair in range(pairs):
                a, b = mine[y, pair], other[y, pair]
                both = jnp.concatenate([jnp.where(low, a, b), jnp.where(low, b, a)])
                at = (y * pairs + pair) * 2 * columns
                out[:, at : at + 2 * columns] = both.T

    return pl.pallas_call(
        kernel,
        in_specs=[SMALL] + [pl.BlockSpec(memory_space=pltpu.VMEM)] * 2,
        out_shape=jax.ShapeDtypeStruct((rows, 2 * columns * ys * pairs), bf16),
        compiler_params=pltpu.CompilerParams(vmem_limit_bytes=LIMIT),
        cost_estimate=LIGHT,
        name="weave",
    )(core, *[pltpu.with_memory_space_constraint(v, pltpu.VMEM) for v in (mine, other)])


class Outer:
    def __init__(self, fragment_local, global_params, outer_moment, fragment):
        me = lax.axis_index("rep").astype(jnp.int32).reshape(1)
        self.far, self.near, self.pair, self.core = me // 8, me // 4 % 2, me // 2 % 2, me % 2
        self.index = fragment
        self.local = fragment_local[0]
        self.globs = jnp.swapaxes(global_params, 1, 2)
        self.outers = jnp.swapaxes(outer_moment, 1, 2)

    def swap_params(self, *since):
        own = chosen_params(*tie([self.globs, self.outers], *since), self.index)
        self.params = (own, swap_pair(own))

    def swap_cores(self, *since):
        mine, other = turn_fragment(tie([self.local], *since)[0], self.core)
        self.state = (mine, swap_core(other))

    def reduce_far(self, *since):
        mine, other = halve(*tie(self.state, *since), self.far, "halve_far")
        self.state = (mine, swap_far(other))

    def reduce_near(self, *since):
        mine, other = halve(*tie(self.state, *since), self.near, "halve_near")
        self.state = (mine[0], swap_near(other)[0])

    def reduce_pair(self, *since):
        mine = total(*tie(self.state, *since))
        self.state = (mine, swap_pair(mine))

    def gather_near(self, *since):
        mine, other = tie(self.state, *since)
        updated, self.new_global, self.new_outer = nesterov(
            mine,
            other,
            *self.params,
            self.globs,
            self.outers,
            self.index,
            self.pair,
            lax.axis_size("rep"),
        )
        updated = updated[None]
        self.state = (updated, swap_near(updated))

    def gather_far(self, *since):
        both = stack(*tie(self.state, *since), self.near, "stack_near")
        self.state = (both, swap_far(both))

    def gather_cores(self, *since):
        both = stack(*tie(self.state, *since), self.far, "stack_far")
        self.state = (both, swap_core(both))

    def results(self):
        return (
            weave(*self.state, self.core)[None],
            jnp.swapaxes(self.new_global, 1, 2),
            jnp.swapaxes(self.new_outer, 1, 2),
        )


def tie(values, *others):
    return lax.optimization_barrier((tuple(values), others))[0]


def body(
    tokens,
    targets,
    weight,
    moment_first,
    moment_second,
    fragment_local,
    global_params,
    outer_moment,
    fragment,
):
    outer = Outer(fragment_local, global_params, outer_moment, fragment)
    shard = weight[0]
    width = tokens.shape[1]
    inv_root = 1.0 / math.sqrt(width)
    scale = 1.0 / math.sqrt(tokens.shape[0] * lax.axis_size("fsdp"))

    owns = split_columns(shard, CHUNKS)
    blocks = [[own, along_z(own, -1), along_z(own, 1)] for own in owns]
    pieces = pack_tokens(tokens)
    far = {k: along_x(pieces[k], k) for k in (2, 1, 3)}
    pieces = [pieces[0], far[1], far[2], far[3]]
    def pass_on(block):
        own, following, previous = block
        top, bottom = outer_halves(previous, following)
        return [own, following, along_z(top, 1), along_z(bottom, -1), previous]

    def back(keys):
        return {k: along_x(keys[k], -k) for k in (2, 1, 3)}

    def out(keys, got, part):
        resid = residual(keys[0], [got[1], got[2], got[3]], targets, part, inv_root)
        there = {k: along_x(resid, k) for k in (2, 1, 3)}
        return [resid, there[1], there[2], there[3]]

    outer.swap_params(blocks[0][2])
    keys = partial_keys(pieces, pass_on(blocks[0]), HEAVY)
    got = back(keys)
    outer.swap_cores(keys[0])
    outer.reduce_far()
    block = pass_on(tie(blocks[1], got[1]))
    turned = transpose_tokens(tie(pieces, keys[0]))
    resids = out(keys, got, 0)
    outer.reduce_near()

    keys = partial_keys(pieces, tie(block, resids[0]), HEAVY)
    got = back(keys)
    outer.reduce_pair(*block)
    outer.gather_near()
    outer.gather_far()

    own, one, far_a, far_b, three = partial_grad(turned, resids)
    far_a, far_b = along_z(far_a, 1), along_z(far_b, -1)
    resids = out(keys, got, 1)

    up, down = add_halves(one, far_a, three, far_b)
    left, right = along_z(up, 1), along_z(down, -1)
    outer.gather_cores(up)

    own1, one1, far_a, far_b, three1 = partial_grad(turned, tie(resids, up))
    far_a, far_b = along_z(far_a, 1), along_z(far_b, -1)
    staged = load(tie([shard, moment_first[0], moment_second[0]], own1), "load_state")

    up, down = add_halves(one1, far_a, three1, far_b)
    left1, right1 = along_z(up, 1), along_z(down, -1)
    outs = adam_columns(0, CHUNKS, scale, own, left, right, *staged, None)
    outs = adam_columns(1, CHUNKS, scale, own1, left1, right1, *staged, outs)
    new_weight, new_first, new_second = outs
    return (new_weight[None], new_first[None], new_second[None], *outer.results())


def solution(mesh):
    return jax.shard_map(
        body,
        mesh=mesh,
        in_specs=(
            P(("rep", "fsdp"), None),
            P(("rep", "fsdp"), None),
            P("rep", "fsdp", None),
            P("rep", "fsdp", None),
            P("rep", "fsdp", None),
            P("rep", "fsdp", None),
            P(None, "fsdp", "rep"),
            P(None, "fsdp", "rep"),
            P(),
        ),
        out_specs=(
            P("rep", "fsdp", None),
            P("rep", "fsdp", None),
            P("rep", "fsdp", None),
            P("rep", "fsdp", None),
            P(None, "fsdp", "rep"),
            P(None, "fsdp", "rep"),
        ),
        check_vma=False,
    )
```

profile of v0, /device:TPU:16, one launch (start us, length us, event | category | flops | bytes accessed | tf_op | source)
XLA Modules:
  0.0 167.2 jit_solution(3394522241359286083)
XLA Ops:
  0.6 1.9 %copy-done = bf16[256,6144]{1,0:T(8,128)(2,1)S(1)} copy-done((bf16[256,6144]{1,0:T(8,128)(2,1)S(1)}, bf16[256,6144]{1,0:T(8,128)(2,1)}, u32[]{:S(2)}) %copy-start) | copy-done | bytes 3145752
  2.5 0.6 pack_tokens.1
  3.2 1.6 collective-permute-start
  4.7 2.7 %collective-permute-start.1 = (bf16[256,1536]{1,0:T(8,128)(2,1)S(1)}, bf16[256,1536]{1,0:T(8,128)(2,1)S(1)}, u32[]{:S(2)}, u32[]{:S(2)}) collective-permute-start(bf16[256,1536]{1,0:T(8,128)(2,1)S(1)} %get-tuple-element.92), channel_id=1, source_target_pairs={{0,2},{1,3},{2,0},{3,1},{4,6},{5,7},{6,4},{7,5},{8,10},{9,11},{10,... | collective-permute-start | bytes 2359304 | tf_op jit(solution)/shard_map/ppermute | solution.py:24
  7.5 1.4 collective-permute-start.2
  9.0 3.3 %collective-permute-start.4 = (bf16[384,512]{1,0:T(8,128)(2,1)S(1)}, bf16[384,512]{1,0:T(8,128)(2,1)S(1)}, u32[]{:S(2)}, u32[]{:S(2)}) collective-permute-start(bf16[384,512]{1,0:T(8,128)(2,1)S(1)} %get-tuple-element.94.refs_4_), channel_id=1, source_target_pairs={{0,4},{1,5},{2,6},{3,7},{4,8},{5,9},{6,10},{7,11},{8,12},{9,13},{1... | collective-permute-start | bytes 1179656 | tf_op jit(solution)/shard_map/ppermute | solution.py:29
  12.3 3.1 %collective-permute-start.3 = (bf16[384,512]{1,0:T(8,128)(2,1)S(1)}, bf16[384,512]{1,0:T(8,128)(2,1)S(1)}, u32[]{:S(2)}, u32[]{:S(2)}) collective-permute-start(bf16[384,512]{1,0:T(8,128)(2,1)S(1)} %get-tuple-element.94.refs_4_), channel_id=1, source_target_pairs={{0,12},{1,13},{2,14},{3,15},{4,0},{5,1},{6,2},{7,3},{8,4},{9,5},{1... | collective-permute-start | bytes 1179656 | tf_op jit(solution)/shard_map/ppermute | solution.py:29
  15.4 11.2 %collective-permute-done.4.previous.refs_8_ = bf16[384,512]{1,0:T(8,128)(2,1)S(1)} collective-permute-done((bf16[384,512]{1,0:T(8,128)(2,1)S(1)}, bf16[384,512]{1,0:T(8,128)(2,1)S(1)}, u32[]{:S(2)}, u32[]{:S(2)}) %collective-permute-start.4) | collective-permute-done | bytes 393248 | tf_op jit(solution)/shard_map/ppermute | solution.py:29
  26.6 6.6 %collective-permute-done.3.following.refs_5_ = bf16[384,512]{1,0:T(8,128)(2,1)S(1)} collective-permute-done((bf16[384,512]{1,0:T(8,128)(2,1)S(1)}, bf16[384,512]{1,0:T(8,128)(2,1)S(1)}, u32[]{:S(2)}, u32[]{:S(2)}) %collective-permute-start.3) | collective-permute-done | bytes 393248 | tf_op jit(solution)/shard_map/ppermute | solution.py:29
  33.3 3.8 %collective-permute-start.5 = (bf16[192,512]{1,0:T(8,128)(2,1)S(1)}, bf16[192,512]{1,0:T(8,128)(2,1)S(1)}, u32[]{:S(2)}, u32[]{:S(2)}) collective-permute-start(bf16[192,512]{1,0:T(8,128)(2,1)S(1)} %get-tuple-element.95), channel_id=1, source_target_pairs={{0,4},{1,5},{2,6},{3,7},{4,8},{5,9},{6,10},{7,11},{8,12},{9,13},{1... | collective-permute-start | bytes 589832 | tf_op jit(solution)/shard_map/ppermute | solution.py:29
  37.0 0.4 collective-permute-start.6
  37.5 8.4 %collective-permute-done.5.refs_6_ = bf16[192,512]{1,0:T(8,128)(2,1)S(1)} collective-permute-done((bf16[192,512]{1,0:T(8,128)(2,1)S(1)}, bf16[192,512]{1,0:T(8,128)(2,1)S(1)}, u32[]{:S(2)}, u32[]{:S(2)}) %collective-permute-start.5) | collective-permute-done | bytes 196640 | tf_op jit(solution)/shard_map/ppermute | solution.py:29
  45.9 2.4 %collective-permute-start.8 = (bf16[384,512]{1,0:T(8,128)(2,1)S(1)}, bf16[384,512]{1,0:T(8,128)(2,1)S(1)}, u32[]{:S(2)}, u32[]{:S(2)}) collective-permute-start(bf16[384,512]{1,0:T(8,128)(2,1)S(1)} %get-tuple-element.111.refs_4_), channel_id=1, source_target_pairs={{0,4},{1,5},{2,6},{3,7},{4,8},{5,9},{6,10},{7,11},{8,12},{9,13},{1... | collective-permute-start | bytes 1179656 | tf_op jit(solution)/shard_map/ppermute | solution.py:29
  48.2 1.8 %collective-permute-start.7 = (bf16[384,512]{1,0:T(8,128)(2,1)S(1)}, bf16[384,512]{1,0:T(8,128)(2,1)S(1)}, u32[]{:S(2)}, u32[]{:S(2)}) collective-permute-start(bf16[384,512]{1,0:T(8,128)(2,1)S(1)} %get-tuple-element.111.refs_4_), channel_id=1, source_target_pairs={{0,12},{1,13},{2,14},{3,15},{4,0},{5,1},{6,2},{7,3},{8,4},{9,5},{1... | collective-permute-start | bytes 1179656 | tf_op jit(solution)/shard_map/ppermute | solution.py:29
  50.1 2.3 %partial_keys.2 = (f32[256,512]{1,0:T(8,128)S(1)}, bf16[256,512]{1,0:T(8,128)(2,1)}, bf16[256,512]{1,0:T(8,128)(2,1)S(1)}, bf16[256,512]{1,0:T(8,128)(2,1)S(1)}) custom-call(bf16[256,1536]{1,0:T(8,128)(2,1)S(1)} %get-tuple-element.98.refs_0_, bf16[256,1536]{1,0:T(8,128)(2,1)S(1)} %collective-permute-done.refs_1_, ...), custom_call_target="tpu_custom_call" | custom-call | flops 40000000000 | bytes 1000000 | tf_op jit(solution)/shard_map/partial_keys/pallas_call | solution.py:57
  52.3 0.7 copy-done.13
  53.0 0.7 copy-done.14
  53.7 0.3 collective-permute-start.9
  54.0 2.4 %collective-permute-start.12 = (bf16[256,512]{1,0:T(8,128)(2,1)}, bf16[256,512]{1,0:T(8,128)(2,1)S(1)}, u32[]{:S(2)}, u32[]{:S(2)}) collective-permute-start(bf16[256,512]{1,0:T(8,128)(2,1)} %copy-done.14), channel_id=1, source_target_pairs={{0,2},{1,3},{2,0},{3,1},{4,6},{5,7},{6,4},{7,5},{8,10},{9,11},{10,... | collective-permute-start | bytes 786440 | tf_op jit(solution)/shard_map/ppermute | solution.py:24
  56.4 0.3 turn_fragment.1
  56.7 5.5 %collective-permute-done.8.previous.refs_8_ = bf16[384,512]{1,0:T(8,128)(2,1)S(1)} collective-permute-done((bf16[384,512]{1,0:T(8,128)(2,1)S(1)}, bf16[384,512]{1,0:T(8,128)(2,1)S(1)}, u32[]{:S(2)}, u32[]{:S(2)}) %collective-permute-start.8) | collective-permute-done | bytes 393248 | tf_op jit(solution)/shard_map/ppermute | solution.py:29
  62.2 0.7 collective-permute-done.7.following.refs_5_
  62.9 0.3 collective-permute-done.9.one
  63.2 1.6 collective-permute-start.10
  64.8 2.8 %collective-permute-start.11 = (bf16[192,512]{1,0:T(8,128)(2,1)S(1)}, bf16[192,512]{1,0:T(8,128)(2,1)S(1)}, u32[]{:S(2)}, u32[]{:S(2)}) collective-permute-start(bf16[192,512]{1,0:T(8,128)(2,1)S(1)} %get-tuple-element.108), channel_id=1, source_target_pairs={{0,12},{1,13},{2,14},{3,15},{4,0},{5,1},{6,2},{7,3},{8,4},{9,5},{1... | collective-permute-start | bytes 589832 | tf_op jit(solution)/shard_map/ppermute | solution.py:29
  67.6 1.1 copy-done.11
  68.8 0.9 transpose_tokens.1.turned_ref
  69.7 0.2 residual.2.refs_0_
  69.9 0.4 collective-permute-start.22
  70.3 6.4 %collective-permute-start.21 = (bf16[256,512]{1,0:T(8,128)(2,1)S(1)}, bf16[256,512]{1,0:T(8,128)(2,1)S(1)}, u32[]{:S(2)}, u32[]{:S(2)}) collective-permute-start(bf16[256,512]{1,0:T(8,128)(2,1)S(1)} %residual.2.refs_0_), channel_id=1, source_target_pairs={{0,2},{1,3},{2,0},{3,1},{4,6},{5,7},{6,4},{7,5},{8,10},{9,11},{10,... | collective-permute-start | bytes 786440 | tf_op jit(solution)/shard_map/ppermute | solution.py:24
  76.8 0.4 collective-permute-start.32
  77.2 1.8 %partial_keys.3 = (f32[256,512]{1,0:T(8,128)S(1)}, bf16[256,512]{1,0:T(8,128)(2,1)S(1)}, bf16[256,512]{1,0:T(8,128)(2,1)S(1)}, bf16[256,512]{1,0:T(8,128)(2,1)S(1)}) custom-call(bf16[256,1536]{1,0:T(8,128)(2,1)S(1)} %get-tuple-element.98.refs_0_, bf16[256,1536]{1,0:T(8,128)(2,1)S(1)} %copy-done.7, bf16[256,1536]{1,0:T(8,128)(2,1)S(1)} %copy-done.9, ...), custom_call_target="tpu_custom_call" | custom-call | flops 40000000000 | bytes 1000000 | tf_op jit(solution)/shard_map/partial_keys/pallas_call | solution.py:57
  79.0 3.3 %collective-permute-start.14 = (bf16[256,512]{1,0:T(8,128)(2,1)S(1)}, bf16[256,512]{1,0:T(8,128)(2,1)S(1)}, u32[]{:S(2)}, u32[]{:S(2)}) collective-permute-start(bf16[256,512]{1,0:T(8,128)(2,1)S(1)} %get-tuple-element.117), channel_id=1, source_target_pairs={{0,3},{1,0},{2,1},{3,2},{4,7},{5,4},{6,5},{7,6},{8,11},{9,8},{10,9... | collective-permute-start | bytes 786440 | tf_op jit(solution)/shard_map/ppermute | solution.py:24
  82.3 4.5 %collective-permute-done.32.other = f32[2,2,64,384]{3,2,1,0:T(8,128)S(1)} collective-permute-done((f32[2,2,64,384]{3,2,1,0:T(8,128)S(1)}, f32[2,2,64,384]{3,2,1,0:T(8,128)S(1)}, u32[]{:S(2)}, u32[]{:S(2)}) %collective-permute-start.32) | collective-permute-done | bytes 393248 | tf_op jit(solution)/shard_map/ppermute | solution.py:37
  86.9 2.3 %collective-permute-start.15 = (bf16[256,512]{1,0:T(8,128)(2,1)S(1)}, bf16[256,512]{1,0:T(8,128)(2,1)S(1)}, u32[]{:S(2)}, u32[]{:S(2)}) collective-permute-start(bf16[256,512]{1,0:T(8,128)(2,1)S(1)} %get-tuple-element.118), channel_id=1, source_target_pairs={{0,2},{1,3},{2,0},{3,1},{4,6},{5,7},{6,4},{7,5},{8,10},{9,11},{10,... | collective-permute-start | bytes 786440 | tf_op jit(solution)/shard_map/ppermute | solution.py:24
  89.3 2.2 %collective-permute-start.16 = (bf16[256,512]{1,0:T(8,128)(2,1)S(1)}, bf16[256,512]{1,0:T(8,128)(2,1)S(1)}, u32[]{:S(2)}, u32[]{:S(2)}) collective-permute-start(bf16[256,512]{1,0:T(8,128)(2,1)S(1)} %get-tuple-element.119), channel_id=1, source_target_pairs={{0,1},{1,2},{2,3},{3,0},{4,5},{5,6},{6,7},{7,4},{8,9},{9,10},{10,1... | collective-permute-start | bytes 786440 | tf_op jit(solution)/shard_map/ppermute | solution.py:24
  91.5 1.7 %collective-permute-start.33 = (f32[1,2,64,384]{3,2,1,0:T(8,128)S(1)}, f32[1,2,64,384]{3,2,1,0:T(8,128)S(1)}, u32[]{:S(2)}, u32[]{:S(2)}) collective-permute-start(f32[1,2,64,384]{3,2,1,0:T(8,128)S(1)} %get-tuple-element.160), channel_id=1, source_target_pairs={{0,64},{16,80},{32,96},{48,112},{64,0},{80,16},{96,32},{112,48},{1... | collective-permute-start | bytes 589832 | tf_op jit(solution)/shard_map/ppermute | solution.py:33
  93.2 1.8 %partial_grad.2 = (f32[384,512]{1,0:T(8,128)S(1)}, bf16[384,512]{1,0:T(8,128)(2,1)S(1)}, bf16[192,512]{1,0:T(8,128)(2,1)S(1)}, bf16[192,512]{1,0:T(8,128)(2,1)S(1)}, bf16[384,512]{1,0:T(8,128)(2,1)S(1)}) custom-call(bf16[1536,1024]{1,0:T(8,128)(2,1)S(1)} %transpose_tokens.1.turned_ref, bf16[256,512]{1,0:T(8,128)(2,1)S(1)} %residual.2.refs_0_, ...), custom_call_target="tpu_custom_call" | custom-call | flops 40000000000 | bytes 1000000 | tf_op jit(solution)/shard_map/partial_grad/pallas_call | solution.py:57
  95.1 4.1 %collective-permute-start.24 = (bf16[192,512]{1,0:T(8,128)(2,1)S(1)}, bf16[192,512]{1,0:T(8,128)(2,1)S(1)}, u32[]{:S(2)}, u32[]{:S(2)}) collective-permute-start(bf16[192,512]{1,0:T(8,128)(2,1)S(1)} %get-tuple-element.123), channel_id=1, source_target_pairs={{0,12},{1,13},{2,14},{3,15},{4,0},{5,1},{6,2},{7,3},{8,4},{9,5},{1... | collective-permute-start | bytes 589832 | tf_op jit(solution)/shard_map/ppermute | solution.py:29
  99.2 1.9 %collective-permute-done.16.three = bf16[256,512]{1,0:T(8,128)(2,1)S(1)} collective-permute-done((bf16[256,512]{1,0:T(8,128)(2,1)S(1)}, bf16[256,512]{1,0:T(8,128)(2,1)S(1)}, u32[]{:S(2)}, u32[]{:S(2)}) %collective-permute-start.16) | collective-permute-done | bytes 262176 | tf_op jit(solution)/shard_map/ppermute | solution.py:24
  101.1 0.2 residual.3.refs_0_
  101.3 3.6 %collective-permute-start.18 = (bf16[256,512]{1,0:T(8,128)(2,1)S(1)}, bf16[256,512]{1,0:T(8,128)(2,1)S(1)}, u32[]{:S(2)}, u32[]{:S(2)}) collective-permute-start(bf16[256,512]{1,0:T(8,128)(2,1)S(1)} %residual.3.refs_0_), channel_id=1, source_target_pairs={{0,2},{1,3},{2,0},{3,1},{4,6},{5,7},{6,4},{7,5},{8,10},{9,11},{10,... | collective-permute-start | bytes 786440 | tf_op jit(solution)/shard_map/ppermute | solution.py:24
  105.0 1.3 collective-permute-start.17
  107.1 2.1 %collective-permute-start.35 = (f32[2,64,384]{2,1,0:T(8,128)S(1)}, f32[2,64,384]{2,1,0:T(8,128)S(1)}, u32[]{:S(2)}, u32[]{:S(2)}) collective-permute-start(f32[2,64,384]{2,1,0:T(8,128)S(1)} %chosen_params.1.own), channel_id=1, source_target_pairs={{0,32},{16,48},{32,0},{48,16},{64,96},{80,112},{96,64},{112,80},{1... | collective-permute-start | bytes 589832 | tf_op jit(solution)/shard_map/ppermute | solution.py:45
  109.2 0.1 add_halves.2
  109.3 3.2 %collective-permute-done.17.refs_1_ = bf16[256,512]{1,0:T(8,128)(2,1)S(1)} collective-permute-done((bf16[256,512]{1,0:T(8,128)(2,1)S(1)}, bf16[256,512]{1,0:T(8,128)(2,1)S(1)}, u32[]{:S(2)}, u32[]{:S(2)}) %collective-permute-start.17) | collective-permute-done | bytes 262176 | tf_op jit(solution)/shard_map/ppermute | solution.py:24
  112.5 0.2 collective-permute-done.34.other
  112.7 2.1 %collective-permute-done.35.theirs = f32[2,64,384]{2,1,0:T(8,128)S(1)} collective-permute-done((f32[2,64,384]{2,1,0:T(8,128)S(1)}, f32[2,64,384]{2,1,0:T(8,128)S(1)}, u32[]{:S(2)}, u32[]{:S(2)}) %collective-permute-start.35) | collective-permute-done | bytes 196640 | tf_op jit(solution)/shard_map/ppermute | solution.py:45
  114.8 0.8 nesterov.1
  115.6 1.7 %collective-permute-start.36 = (bf16[1,2,64,384]{3,2,1,0:T(8,128)(2,1)S(1)}, bf16[1,2,64,384]{3,2,1,0:T(8,128)(2,1)S(1)}, u32[]{:S(2)}, u32[]{:S(2)}) collective-permute-start(bf16[1,2,64,384]{3,2,1,0:T(8,128)(2,1)S(1)} %bitcast.26), channel_id=1, source_target_pairs={{0,64},{16,80},{32,96},{48,112},{64,0},{80,16},{96,32},{112,48},{1... | collective-permute-start | bytes 294920 | tf_op jit(solution)/shard_map/ppermute | solution.py:33
  117.3 1.8 %partial_grad.3 = (f32[384,512]{1,0:T(8,128)S(1)}, bf16[384,512]{1,0:T(8,128)(2,1)S(1)}, bf16[192,512]{1,0:T(8,128)(2,1)S(1)}, bf16[192,512]{1,0:T(8,128)(2,1)S(1)}, bf16[384,512]{1,0:T(8,128)(2,1)S(1)}) custom-call(bf16[1536,1024]{1,0:T(8,128)(2,1)S(1)} %transpose_tokens.1.turned_ref, bf16[256,512]{1,0:T(8,128)(2,1)S(1)} %residual.3.refs_0_, ...), custom_call_target="tpu_custom_call" | custom-call | flops 40000000000 | bytes 1000000 | tf_op jit(solution)/shard_map/partial_grad/pallas_call | solution.py:57
  119.2 4.1 %collective-permute-start.26 = (bf16[192,512]{1,0:T(8,128)(2,1)S(1)}, bf16[192,512]{1,0:T(8,128)(2,1)S(1)}, u32[]{:S(2)}, u32[]{:S(2)}) collective-permute-start(bf16[192,512]{1,0:T(8,128)(2,1)S(1)} %get-tuple-element.133), channel_id=1, source_target_pairs={{0,12},{1,13},{2,14},{3,15},{4,0},{5,1},{6,2},{7,3},{8,4},{9,5},{1... | collective-permute-start | bytes 589832 | tf_op jit(solution)/shard_map/ppermute | solution.py:29
  123.6 4.1 %collective-permute-start.30 = (bf16[384,512]{1,0:T(8,128)(2,1)S(1)}, bf16[384,512]{1,0:T(8,128)(2,1)S(1)}, u32[]{:S(2)}, u32[]{:S(2)}) collective-permute-start(bf16[384,512]{1,0:T(8,128)(2,1)S(1)} %get-tuple-element.143), channel_id=1, source_target_pairs={{0,12},{1,13},{2,14},{3,15},{4,0},{5,1},{6,2},{7,3},{8,4},{9,5},{1... | collective-permute-start | bytes 1179656 | tf_op jit(solution)/shard_map/ppermute | solution.py:29
  127.7 6.2 %collective-permute-done.25.far_a = bf16[192,512]{1,0:T(8,128)(2,1)S(1)} collective-permute-done((bf16[192,512]{1,0:T(8,128)(2,1)S(1)}, bf16[192,512]{1,0:T(8,128)(2,1)S(1)}, u32[]{:S(2)}, u32[]{:S(2)}) %collective-permute-start.25) | collective-permute-done | bytes 196640 | tf_op jit(solution)/shard_map/ppermute | solution.py:29
  134.0 1.6 collective-permute-start.27
  135.6 2.8 %collective-permute-start.28 = (bf16[384,512]{1,0:T(8,128)(2,1)S(1)}, bf16[384,512]{1,0:T(8,128)(2,1)S(1)}, u32[]{:S(2)}, u32[]{:S(2)}) collective-permute-start(bf16[384,512]{1,0:T(8,128)(2,1)S(1)} %get-tuple-element.135), channel_id=1, source_target_pairs={{0,12},{1,13},{2,14},{3,15},{4,0},{5,1},{6,2},{7,3},{8,4},{9,5},{1... | collective-permute-start | bytes 1179656 | tf_op jit(solution)/shard_map/ppermute | solution.py:29
  138.5 2.2 %load_state.1 = (bf16[384,1024]{1,0:T(8,128)(2,1)S(1)}, f32[384,1024]{1,0:T(8,128)S(1)}, f32[384,1024]{1,0:T(8,128)S(1)}) custom-call(bf16[384,1024]{1,0:T(8,128)(2,1)} %bitcast.17, f32[384,1024]{1,0:T(8,128)} %bitcast.30, f32[384,1024]{1,0:T(8,128)} %bitcast.31), custom_call_target="tpu_custom_call" | custom-call | flops 1 | bytes 1 | tf_op jit(solution)/shard_map/load_state/pallas_call | solution.py:57
  140.7 7.9 %collective-permute-done.30.right = bf16[384,512]{1,0:T(8,128)(2,1)S(1)} collective-permute-done((bf16[384,512]{1,0:T(8,128)(2,1)S(1)}, bf16[384,512]{1,0:T(8,128)(2,1)S(1)}, u32[]{:S(2)}, u32[]{:S(2)}) %collective-permute-start.30) | collective-permute-done | bytes 393248 | tf_op jit(solution)/shard_map/ppermute | solution.py:29
  148.6 3.8 %collective-permute-done.29.left = bf16[384,512]{1,0:T(8,128)(2,1)S(1)} collective-permute-done((bf16[384,512]{1,0:T(8,128)(2,1)S(1)}, bf16[384,512]{1,0:T(8,128)(2,1)S(1)}, u32[]{:S(2)}, u32[]{:S(2)}) %collective-permute-start.29) | collective-permute-done | bytes 393248 | tf_op jit(solution)/shard_map/ppermute | solution.py:29
  152.4 2.1 %adam_columns.2 = (bf16[384,1024]{1,0:T(8,128)(2,1)}, f32[384,1024]{1,0:T(8,128)}, f32[384,1024]{1,0:T(8,128)}) custom-call(f32[384,512]{1,0:T(8,128)S(1)} %get-tuple-element.142.own, bf16[384,512]{1,0:T(8,128)(2,1)S(1)} %collective-permute-done.29.left, bf16[384,512]{1,0:T(8,128)(2,1)S(1)} %collective-permute-done.30.right, ...), custom_call_target="tpu_custom_call" | custom-call | flops 1 | bytes 1 | tf_op jit(solution)/shard_map/adam_columns/pallas_call | solution.py:300
  154.5 6.5 %collective-permute-done.27.left = bf16[384,512]{1,0:T(8,128)(2,1)S(1)} collective-permute-done((bf16[384,512]{1,0:T(8,128)(2,1)S(1)}, bf16[384,512]{1,0:T(8,128)(2,1)S(1)}, u32[]{:S(2)}, u32[]{:S(2)}) %collective-permute-start.27) | collective-permute-done | bytes 393248 | tf_op jit(solution)/shard_map/ppermute | solution.py:29
  161.1 2.9 %collective-permute-done.28.right = bf16[384,512]{1,0:T(8,128)(2,1)S(1)} collective-permute-done((bf16[384,512]{1,0:T(8,128)(2,1)S(1)}, bf16[384,512]{1,0:T(8,128)(2,1)S(1)}, u32[]{:S(2)}, u32[]{:S(2)}) %collective-permute-start.28) | collective-permute-done | bytes 393248 | tf_op jit(solution)/shard_map/ppermute | solution.py:29
  164.0 2.1 %adam_columns.3 = (bf16[384,1024]{1,0:T(8,128)(2,1)}, f32[384,1024]{1,0:T(8,128)}, f32[384,1024]{1,0:T(8,128)}) custom-call(f32[384,512]{1,0:T(8,128)S(1)} %get-tuple-element.129.own, bf16[384,512]{1,0:T(8,128)(2,1)S(1)} %collective-permute-done.27.left, ...), custom_call_target="tpu_custom_call", output_to_operand_aliasing={{0}: (6, {}), {1}: (7, {}), {2}: (8, {})} | custom-call | flops 1 | bytes 1 | tf_op jit(solution)/shard_map/adam_columns/pallas_call | solution.py:300
  166.1 1.2 weave.1
  (69 shorter events, 1.2 us)
Async XLA Ops:
  0.6 1.9 %copy-start = (bf16[256,6144]{1,0:T(8,128)(2,1)S(1)}, bf16[256,6144]{1,0:T(8,128)(2,1)}, u32[]{:S(2)}) copy-start(bf16[256,6144]{1,0:T(8,128)(2,1)} %source.1) | copy-start | bytes 9437188
  2.5 6.4 %copy-start.1 = (bf16[1,384,1024]{2,1,0:T(8,128)(2,1)S(1)}, bf16[1,384,1024]{2,1,0:T(8,128)(2,1)}, u32[]{:S(2)}) copy-start(bf16[1,384,1024]{2,1,0:T(8,128)(2,1)} %param.11) | copy-start | bytes 2359300
  3.2 46.9 %collective-permute-start = (bf16[256,1536]{1,0:T(8,128)(2,1)S(1)}, bf16[256,1536]{1,0:T(8,128)(2,1)S(1)}, u32[]{:S(2)}, u32[]{:S(2)}) collective-permute-start(bf16[256,1536]{1,0:T(8,128)(2,1)S(1)} %get-tuple-element.91), channel_id=1, source_target_pairs={{0,1},{1,2},{2,3},{3,0},{4,5},{5,6},{6,7},{7,4},{8,9},{9,10},{10,1... | collective-permute-start | bytes 2359304 | tf_op jit(solution)/shard_map/ppermute | solution.py:24
  4.7 45.3 %collective-permute-start.1 = (bf16[256,1536]{1,0:T(8,128)(2,1)S(1)}, bf16[256,1536]{1,0:T(8,128)(2,1)S(1)}, u32[]{:S(2)}, u32[]{:S(2)}) collective-permute-start(bf16[256,1536]{1,0:T(8,128)(2,1)S(1)} %get-tuple-element.92), channel_id=1, source_target_pairs={{0,2},{1,3},{2,0},{3,1},{4,6},{5,7},{6,4},{7,5},{8,10},{9,11},{10,... | collective-permute-start | bytes 2359304 | tf_op jit(solution)/shard_map/ppermute | solution.py:24
  7.5 42.6 %collective-permute-start.2 = (bf16[256,1536]{1,0:T(8,128)(2,1)S(1)}, bf16[256,1536]{1,0:T(8,128)(2,1)S(1)}, u32[]{:S(2)}, u32[]{:S(2)}) collective-permute-start(bf16[256,1536]{1,0:T(8,128)(2,1)S(1)} %get-tuple-element.93), channel_id=1, source_target_pairs={{0,3},{1,0},{2,1},{3,2},{4,7},{5,4},{6,5},{7,6},{8,11},{9,8},{10,9... | collective-permute-start | bytes 2359304 | tf_op jit(solution)/shard_map/ppermute | solution.py:24
  9.0 17.6 %collective-permute-start.4 = (bf16[384,512]{1,0:T(8,128)(2,1)S(1)}, bf16[384,512]{1,0:T(8,128)(2,1)S(1)}, u32[]{:S(2)}, u32[]{:S(2)}) collective-permute-start(bf16[384,512]{1,0:T(8,128)(2,1)S(1)} %get-tuple-element.94.refs_4_), channel_id=1, source_target_pairs={{0,4},{1,5},{2,6},{3,7},{4,8},{5,9},{6,10},{7,11},{8,12},{9,13},{1... | collective-permute-start | bytes 1179656 | tf_op jit(solution)/shard_map/ppermute | solution.py:29
  12.3 20.9 %collective-permute-start.3 = (bf16[384,512]{1,0:T(8,128)(2,1)S(1)}, bf16[384,512]{1,0:T(8,128)(2,1)S(1)}, u32[]{:S(2)}, u32[]{:S(2)}) collective-permute-start(bf16[384,512]{1,0:T(8,128)(2,1)S(1)} %get-tuple-element.94.refs_4_), channel_id=1, source_target_pairs={{0,12},{1,13},{2,14},{3,15},{4,0},{5,1},{6,2},{7,3},{8,4},{9,5},{1... | collective-permute-start | bytes 1179656 | tf_op jit(solution)/shard_map/ppermute | solution.py:29
  33.3 12.6 %collective-permute-start.5 = (bf16[192,512]{1,0:T(8,128)(2,1)S(1)}, bf16[192,512]{1,0:T(8,128)(2,1)S(1)}, u32[]{:S(2)}, u32[]{:S(2)}) collective-permute-start(bf16[192,512]{1,0:T(8,128)(2,1)S(1)} %get-tuple-element.95), channel_id=1, source_target_pairs={{0,4},{1,5},{2,6},{3,7},{4,8},{5,9},{6,10},{7,11},{8,12},{9,13},{1... | collective-permute-start | bytes 589832 | tf_op jit(solution)/shard_map/ppermute | solution.py:29
  37.0 11.2 %collective-permute-start.6 = (bf16[192,512]{1,0:T(8,128)(2,1)S(1)}, bf16[192,512]{1,0:T(8,128)(2,1)S(1)}, u32[]{:S(2)}, u32[]{:S(2)}) collective-permute-start(bf16[192,512]{1,0:T(8,128)(2,1)S(1)} %get-tuple-element.96), channel_id=1, source_target_pairs={{0,12},{1,13},{2,14},{3,15},{4,0},{5,1},{6,2},{7,3},{8,4},{9,5},{1... | collective-permute-start | bytes 589832 | tf_op jit(solution)/shard_map/ppermute | solution.py:29
  45.9 16.3 %collective-permute-start.8 = (bf16[384,512]{1,0:T(8,128)(2,1)S(1)}, bf16[384,512]{1,0:T(8,128)(2,1)S(1)}, u32[]{:S(2)}, u32[]{:S(2)}) collective-permute-start(bf16[384,512]{1,0:T(8,128)(2,1)S(1)} %get-tuple-element.111.refs_4_), channel_id=1, source_target_pairs={{0,4},{1,5},{2,6},{3,7},{4,8},{5,9},{6,10},{7,11},{8,12},{9,13},{1... | collective-permute-start | bytes 1179656 | tf_op jit(solution)/shard_map/ppermute | solution.py:29
  48.2 14.6 %collective-permute-start.7 = (bf16[384,512]{1,0:T(8,128)(2,1)S(1)}, bf16[384,512]{1,0:T(8,128)(2,1)S(1)}, u32[]{:S(2)}, u32[]{:S(2)}) collective-permute-start(bf16[384,512]{1,0:T(8,128)(2,1)S(1)} %get-tuple-element.111.refs_4_), channel_id=1, source_target_pairs={{0,12},{1,13},{2,14},{3,15},{4,0},{5,1},{6,2},{7,3},{8,4},{9,5},{1... | collective-permute-start | bytes 1179656 | tf_op jit(solution)/shard_map/ppermute | solution.py:29
  50.0 2.3 %copy-start.6 = (bf16[256,1536]{1,0:T(8,128)(2,1)}, bf16[256,1536]{1,0:T(8,128)(2,1)S(1)}, u32[]{:S(2)}) copy-start(bf16[256,1536]{1,0:T(8,128)(2,1)S(1)} %collective-permute-done.refs_1_) | copy-start | bytes 2359300
  50.0 2.3 %copy-start.8 = (bf16[256,1536]{1,0:T(8,128)(2,1)}, bf16[256,1536]{1,0:T(8,128)(2,1)S(1)}, u32[]{:S(2)}) copy-start(bf16[256,1536]{1,0:T(8,128)(2,1)S(1)} %collective-permute-done.1.refs_2_) | copy-start | bytes 2359300
  50.0 2.3 %copy-start.10 = (bf16[256,1536]{1,0:T(8,128)(2,1)}, bf16[256,1536]{1,0:T(8,128)(2,1)S(1)}, u32[]{:S(2)}) copy-start(bf16[256,1536]{1,0:T(8,128)(2,1)S(1)} %collective-permute-done.2.refs_3_) | copy-start | bytes 2359300
  50.1 6.4 %copy-start.3 = (bf16[1,384,1024]{2,1,0:T(8,128)(2,1)S(1)}, bf16[1,384,1024]{2,1,0:T(8,128)(2,1)}, u32[]{:S(2)}) copy-start(bf16[1,384,1024]{2,1,0:T(8,128)(2,1)} %param.14) | copy-start | bytes 2359300
  52.3 0.7 copy-start.13
  53.0 0.7 copy-start.14
  53.7 9.5 %collective-permute-start.9 = (bf16[256,512]{1,0:T(8,128)(2,1)}, bf16[256,512]{1,0:T(8,128)(2,1)S(1)}, u32[]{:S(2)}, u32[]{:S(2)}) collective-permute-start(bf16[256,512]{1,0:T(8,128)(2,1)} %get-tuple-element.103), channel_id=1, source_target_pairs={{0,3},{1,0},{2,1},{3,2},{4,7},{5,4},{6,5},{7,6},{8,11},{9,8},{10,9... | collective-permute-start | bytes 786440 | tf_op jit(solution)/shard_map/ppermute | solution.py:24
  54.0 13.6 %copy-start.7 = (bf16[256,1536]{1,0:T(8,128)(2,1)S(1)}, bf16[256,1536]{1,0:T(8,128)(2,1)}, u32[]{:S(2)}) copy-start(bf16[256,1536]{1,0:T(8,128)(2,1)} %copy-done.6) | copy-start | bytes 2359300
  54.0 13.6 %copy-start.9 = (bf16[256,1536]{1,0:T(8,128)(2,1)S(1)}, bf16[256,1536]{1,0:T(8,128)(2,1)}, u32[]{:S(2)}) copy-start(bf16[256,1536]{1,0:T(8,128)(2,1)} %copy-done.8) | copy-start | bytes 2359300
  54.0 15.7 %collective-permute-start.12 = (bf16[256,512]{1,0:T(8,128)(2,1)}, bf16[256,512]{1,0:T(8,128)(2,1)S(1)}, u32[]{:S(2)}, u32[]{:S(2)}) collective-permute-start(bf16[256,512]{1,0:T(8,128)(2,1)} %copy-done.14), channel_id=1, source_target_pairs={{0,2},{1,3},{2,0},{3,1},{4,6},{5,7},{6,4},{7,5},{8,10},{9,11},{10,... | collective-permute-start | bytes 786440 | tf_op jit(solution)/shard_map/ppermute | solution.py:24
  56.4 13.3 %collective-permute-start.13 = (bf16[256,512]{1,0:T(8,128)(2,1)}, bf16[256,512]{1,0:T(8,128)(2,1)S(1)}, u32[]{:S(2)}, u32[]{:S(2)}) collective-permute-start(bf16[256,512]{1,0:T(8,128)(2,1)} %copy-done.13), channel_id=1, source_target_pairs={{0,1},{1,2},{2,3},{3,0},{4,5},{5,6},{6,7},{7,4},{8,9},{9,10},{10,1... | collective-permute-start | bytes 786440 | tf_op jit(solution)/shard_map/ppermute | solution.py:24
  62.2 14.5 %collective-permute-start.31 = (bf16[4,2,64,384]{3,2,1,0:T(8,128)(2,1)S(1)}, bf16[4,2,64,384]{3,2,1,0:T(8,128)(2,1)S(1)}, u32[]{:S(2)}, u32[]{:S(2)}) collective-permute-start(bf16[4,2,64,384]{3,2,1,0:T(8,128)(2,1)S(1)} %get-tuple-element.152), channel_id=1, source_target_pairs={{0,16},{16,0},{32,48},{48,32},{64,80},{80,64},{96,112},{112,96},{1... | collective-permute-start | bytes 1179656 | tf_op jit(solution)/shard_map/ppermute | solution.py:41
  63.2 13.6 %collective-permute-start.10 = (bf16[192,512]{1,0:T(8,128)(2,1)S(1)}, bf16[192,512]{1,0:T(8,128)(2,1)S(1)}, u32[]{:S(2)}, u32[]{:S(2)}) collective-permute-start(bf16[192,512]{1,0:T(8,128)(2,1)S(1)} %get-tuple-element.107), channel_id=1, source_target_pairs={{0,4},{1,5},{2,6},{3,7},{4,8},{5,9},{6,10},{7,11},{8,12},{9,13},{1... | collective-permute-start | bytes 589832 | tf_op jit(solution)/shard_map/ppermute | solution.py:29
  64.8 4.9 %copy-start.2 = (bf16[256,1024]{1,0:T(8,128)(2,1)S(1)}, bf16[256,1024]{1,0:T(8,128)(2,1)}, u32[]{:S(2)}) copy-start(bf16[256,1024]{1,0:T(8,128)(2,1)} %goals.3) | copy-start | bytes 1572868
  64.8 12.4 %collective-permute-start.11 = (bf16[192,512]{1,0:T(8,128)(2,1)S(1)}, bf16[192,512]{1,0:T(8,128)(2,1)S(1)}, u32[]{:S(2)}, u32[]{:S(2)}) collective-permute-start(bf16[192,512]{1,0:T(8,128)(2,1)S(1)} %get-tuple-element.108), channel_id=1, source_target_pairs={{0,12},{1,13},{2,14},{3,15},{4,0},{5,1},{6,2},{7,3},{8,4},{9,5},{1... | collective-permute-start | bytes 589832 | tf_op jit(solution)/shard_map/ppermute | solution.py:29
  67.6 1.1 copy-start.11
  69.7 7.5 %copy-start.12 = (bf16[256,1536]{1,0:T(8,128)(2,1)S(1)}, bf16[256,1536]{1,0:T(8,128)(2,1)}, u32[]{:S(2)}) copy-start(bf16[256,1536]{1,0:T(8,128)(2,1)} %copy-done.10) | copy-start | bytes 2359300
  69.9 19.3 %collective-permute-start.22 = (bf16[256,512]{1,0:T(8,128)(2,1)S(1)}, bf16[256,512]{1,0:T(8,128)(2,1)S(1)}, u32[]{:S(2)}, u32[]{:S(2)}) collective-permute-start(bf16[256,512]{1,0:T(8,128)(2,1)S(1)} %residual.2.refs_0_), channel_id=1, source_target_pairs={{0,3},{1,0},{2,1},{3,2},{4,7},{5,4},{6,5},{7,6},{8,11},{9,8},{10,9... | collective-permute-start | bytes 786440 | tf_op jit(solution)/shard_map/ppermute | solution.py:24
  70.3 21.2 %collective-permute-start.21 = (bf16[256,512]{1,0:T(8,128)(2,1)S(1)}, bf16[256,512]{1,0:T(8,128)(2,1)S(1)}, u32[]{:S(2)}, u32[]{:S(2)}) collective-permute-start(bf16[256,512]{1,0:T(8,128)(2,1)S(1)} %residual.2.refs_0_), channel_id=1, source_target_pairs={{0,2},{1,3},{2,0},{3,1},{4,6},{5,7},{6,4},{7,5},{8,10},{9,11},{10,... | collective-permute-start | bytes 786440 | tf_op jit(solution)/shard_map/ppermute | solution.py:24
  76.7 16.5 %collective-permute-start.20 = (bf16[256,512]{1,0:T(8,128)(2,1)S(1)}, bf16[256,512]{1,0:T(8,128)(2,1)S(1)}, u32[]{:S(2)}, u32[]{:S(2)}) collective-permute-start(bf16[256,512]{1,0:T(8,128)(2,1)S(1)} %residual.2.refs_0_), channel_id=1, source_target_pairs={{0,1},{1,2},{2,3},{3,0},{4,5},{5,6},{6,7},{7,4},{8,9},{9,10},{10,1... | collective-permute-start | bytes 786440 | tf_op jit(solution)/shard_map/ppermute | solution.py:24
  76.8 10.1 %collective-permute-start.32 = (f32[2,2,64,384]{3,2,1,0:T(8,128)S(1)}, f32[2,2,64,384]{3,2,1,0:T(8,128)S(1)}, u32[]{:S(2)}, u32[]{:S(2)}) collective-permute-start(f32[2,2,64,384]{3,2,1,0:T(8,128)S(1)} %get-tuple-element.156), channel_id=1, source_target_pairs={{0,128},{16,144},{32,160},{48,176},{64,192},{80,208},{96,224},{112... | collective-permute-start | bytes 1179656 | tf_op jit(solution)/shard_map/ppermute | solution.py:37
  79.0 16.1 %collective-permute-start.14 = (bf16[256,512]{1,0:T(8,128)(2,1)S(1)}, bf16[256,512]{1,0:T(8,128)(2,1)S(1)}, u32[]{:S(2)}, u32[]{:S(2)}) collective-permute-start(bf16[256,512]{1,0:T(8,128)(2,1)S(1)} %get-tuple-element.117), channel_id=1, source_target_pairs={{0,3},{1,0},{2,1},{3,2},{4,7},{5,4},{6,5},{7,6},{8,11},{9,8},{10,9... | collective-permute-start | bytes 786440 | tf_op jit(solution)/shard_map/ppermute | solution.py:24
  86.9 12.3 %collective-permute-start.15 = (bf16[256,512]{1,0:T(8,128)(2,1)S(1)}, bf16[256,512]{1,0:T(8,128)(2,1)S(1)}, u32[]{:S(2)}, u32[]{:S(2)}) collective-permute-start(bf16[256,512]{1,0:T(8,128)(2,1)S(1)} %get-tuple-element.118), channel_id=1, source_target_pairs={{0,2},{1,3},{2,0},{3,1},{4,6},{5,7},{6,4},{7,5},{8,10},{9,11},{10,... | collective-permute-start | bytes 786440 | tf_op jit(solution)/shard_map/ppermute | solution.py:24
  89.3 11.8 %collective-permute-start.16 = (bf16[256,512]{1,0:T(8,128)(2,1)S(1)}, bf16[256,512]{1,0:T(8,128)(2,1)S(1)}, u32[]{:S(2)}, u32[]{:S(2)}) collective-permute-start(bf16[256,512]{1,0:T(8,128)(2,1)S(1)} %get-tuple-element.119), channel_id=1, source_target_pairs={{0,1},{1,2},{2,3},{3,0},{4,5},{5,6},{6,7},{7,4},{8,9},{9,10},{10,1... | collective-permute-start | bytes 786440 | tf_op jit(solution)/shard_map/ppermute | solution.py:24
  91.5 13.5 %collective-permute-start.33 = (f32[1,2,64,384]{3,2,1,0:T(8,128)S(1)}, f32[1,2,64,384]{3,2,1,0:T(8,128)S(1)}, u32[]{:S(2)}, u32[]{:S(2)}) collective-permute-start(f32[1,2,64,384]{3,2,1,0:T(8,128)S(1)} %get-tuple-element.160), channel_id=1, source_target_pairs={{0,64},{16,80},{32,96},{48,112},{64,0},{80,16},{96,32},{112,48},{1... | collective-permute-start | bytes 589832 | tf_op jit(solution)/shard_map/ppermute | solution.py:33
  94.9 12.1 %copy-start.4 = (f32[2,384,64]{1,2,0:T(8,128)S(1)}, f32[2,384,64]{1,2,0:T(8,128)}, u32[]{:S(2)}) copy-start(f32[2,384,64]{1,2,0:T(8,128)} %param.15) | copy-start | bytes 589828
  95.0 12.1 %copy-start.5 = (f32[2,384,64]{1,2,0:T(8,128)S(1)}, f32[2,384,64]{1,2,0:T(8,128)}, u32[]{:S(2)}) copy-start(f32[2,384,64]{1,2,0:T(8,128)} %param.16) | copy-start | bytes 589828
  95.0 12.0 %collective-permute-start.23 = (bf16[192,512]{1,0:T(8,128)(2,1)S(1)}, bf16[192,512]{1,0:T(8,128)(2,1)S(1)}, u32[]{:S(2)}, u32[]{:S(2)}) collective-permute-start(bf16[192,512]{1,0:T(8,128)(2,1)S(1)} %get-tuple-element.121), channel_id=1, source_target_pairs={{0,4},{1,5},{2,6},{3,7},{4,8},{5,9},{6,10},{7,11},{8,12},{9,13},{1... | collective-permute-start | bytes 589832 | tf_op jit(solution)/shard_map/ppermute | solution.py:29
  95.1 12.0 %collective-permute-start.24 = (bf16[192,512]{1,0:T(8,128)(2,1)S(1)}, bf16[192,512]{1,0:T(8,128)(2,1)S(1)}, u32[]{:S(2)}, u32[]{:S(2)}) collective-permute-start(bf16[192,512]{1,0:T(8,128)(2,1)S(1)} %get-tuple-element.123), channel_id=1, source_target_pairs={{0,12},{1,13},{2,14},{3,15},{4,0},{5,1},{6,2},{7,3},{8,4},{9,5},{1... | collective-permute-start | bytes 589832 | tf_op jit(solution)/shard_map/ppermute | solution.py:29
  101.3 8.1 %collective-permute-start.19 = (bf16[256,512]{1,0:T(8,128)(2,1)S(1)}, bf16[256,512]{1,0:T(8,128)(2,1)S(1)}, u32[]{:S(2)}, u32[]{:S(2)}) collective-permute-start(bf16[256,512]{1,0:T(8,128)(2,1)S(1)} %residual.3.refs_0_), channel_id=1, source_target_pairs={{0,3},{1,0},{2,1},{3,2},{4,7},{5,4},{6,5},{7,6},{8,11},{9,8},{10,9... | collective-permute-start | bytes 786440 | tf_op jit(solution)/shard_map/ppermute | solution.py:24
  101.3 8.0 %collective-permute-start.18 = (bf16[256,512]{1,0:T(8,128)(2,1)S(1)}, bf16[256,512]{1,0:T(8,128)(2,1)S(1)}, u32[]{:S(2)}, u32[]{:S(2)}) collective-permute-start(bf16[256,512]{1,0:T(8,128)(2,1)S(1)} %residual.3.refs_0_), channel_id=1, source_target_pairs={{0,2},{1,3},{2,0},{3,1},{4,6},{5,7},{6,4},{7,5},{8,10},{9,11},{10,... | collective-permute-start | bytes 786440 | tf_op jit(solution)/shard_map/ppermute | solution.py:24
  105.0 7.6 %collective-permute-start.17 = (bf16[256,512]{1,0:T(8,128)(2,1)S(1)}, bf16[256,512]{1,0:T(8,128)(2,1)S(1)}, u32[]{:S(2)}, u32[]{:S(2)}) collective-permute-start(bf16[256,512]{1,0:T(8,128)(2,1)S(1)} %residual.3.refs_0_), channel_id=1, source_target_pairs={{0,1},{1,2},{2,3},{3,0},{4,5},{5,6},{6,7},{7,4},{8,9},{9,10},{10,1... | collective-permute-start | bytes 786440 | tf_op jit(solution)/shard_map/ppermute | solution.py:24
  107.0 5.8 %collective-permute-start.34 = (f32[2,64,384]{2,1,0:T(8,128)S(1)}, f32[2,64,384]{2,1,0:T(8,128)S(1)}, u32[]{:S(2)}, u32[]{:S(2)}) collective-permute-start(f32[2,64,384]{2,1,0:T(8,128)S(1)} %total.1.mine), channel_id=1, source_target_pairs={{0,32},{16,48},{32,0},{48,16},{64,96},{80,112},{96,64},{112,80},{1... | collective-permute-start | bytes 589832 | tf_op jit(solution)/shard_map/ppermute | solution.py:45
  107.1 7.7 %collective-permute-start.35 = (f32[2,64,384]{2,1,0:T(8,128)S(1)}, f32[2,64,384]{2,1,0:T(8,128)S(1)}, u32[]{:S(2)}, u32[]{:S(2)}) collective-permute-start(f32[2,64,384]{2,1,0:T(8,128)S(1)} %chosen_params.1.own), channel_id=1, source_target_pairs={{0,32},{16,48},{32,0},{48,16},{64,96},{80,112},{96,64},{112,80},{1... | collective-permute-start | bytes 589832 | tf_op jit(solution)/shard_map/ppermute | solution.py:45
  115.6 7.7 %collective-permute-start.36 = (bf16[1,2,64,384]{3,2,1,0:T(8,128)(2,1)S(1)}, bf16[1,2,64,384]{3,2,1,0:T(8,128)(2,1)S(1)}, u32[]{:S(2)}, u32[]{:S(2)}) collective-permute-start(bf16[1,2,64,384]{3,2,1,0:T(8,128)(2,1)S(1)} %bitcast.26), channel_id=1, source_target_pairs={{0,64},{16,80},{32,96},{48,112},{64,0},{80,16},{96,32},{112,48},{1... | collective-permute-start | bytes 294920 | tf_op jit(solution)/shard_map/ppermute | solution.py:33
  119.1 14.8 %collective-permute-start.25 = (bf16[192,512]{1,0:T(8,128)(2,1)S(1)}, bf16[192,512]{1,0:T(8,128)(2,1)S(1)}, u32[]{:S(2)}, u32[]{:S(2)}) collective-permute-start(bf16[192,512]{1,0:T(8,128)(2,1)S(1)} %get-tuple-element.131), channel_id=1, source_target_pairs={{0,4},{1,5},{2,6},{3,7},{4,8},{5,9},{6,10},{7,11},{8,12},{9,13},{1... | collective-permute-start | bytes 589832 | tf_op jit(solution)/shard_map/ppermute | solution.py:29
  119.2 14.7 %collective-permute-start.26 = (bf16[192,512]{1,0:T(8,128)(2,1)S(1)}, bf16[192,512]{1,0:T(8,128)(2,1)S(1)}, u32[]{:S(2)}, u32[]{:S(2)}) collective-permute-start(bf16[192,512]{1,0:T(8,128)(2,1)S(1)} %get-tuple-element.133), channel_id=1, source_target_pairs={{0,12},{1,13},{2,14},{3,15},{4,0},{5,1},{6,2},{7,3},{8,4},{9,5},{1... | collective-permute-start | bytes 589832 | tf_op jit(solution)/shard_map/ppermute | solution.py:29
  123.4 15.0 %collective-permute-start.37 = (bf16[2,2,64,384]{3,2,1,0:T(8,128)(2,1)S(1)}, bf16[2,2,64,384]{3,2,1,0:T(8,128)(2,1)S(1)}, u32[]{:S(2)}, u32[]{:S(2)}) collective-permute-start(bf16[2,2,64,384]{3,2,1,0:T(8,128)(2,1)S(1)} %stack_near.1.mine), channel_id=1, source_target_pairs={{0,128},{16,144},{32,160},{48,176},{64,192},{80,208},{96,224},{112... | collective-permute-start | bytes 589832 | tf_op jit(solution)/shard_map/ppermute | solution.py:37
  123.5 28.9 %collective-permute-start.29 = (bf16[384,512]{1,0:T(8,128)(2,1)S(1)}, bf16[384,512]{1,0:T(8,128)(2,1)S(1)}, u32[]{:S(2)}, u32[]{:S(2)}) collective-permute-start(bf16[384,512]{1,0:T(8,128)(2,1)S(1)} %get-tuple-element.124), channel_id=1, source_target_pairs={{0,4},{1,5},{2,6},{3,7},{4,8},{5,9},{6,10},{7,11},{8,12},{9,13},{1... | collective-permute-start | bytes 1179656 | tf_op jit(solution)/shard_map/ppermute | solution.py:29
  123.6 25.0 %collective-permute-start.30 = (bf16[384,512]{1,0:T(8,128)(2,1)S(1)}, bf16[384,512]{1,0:T(8,128)(2,1)S(1)}, u32[]{:S(2)}, u32[]{:S(2)}) collective-permute-start(bf16[384,512]{1,0:T(8,128)(2,1)S(1)} %get-tuple-element.143), channel_id=1, source_target_pairs={{0,12},{1,13},{2,14},{3,15},{4,0},{5,1},{6,2},{7,3},{8,4},{9,5},{1... | collective-permute-start | bytes 1179656 | tf_op jit(solution)/shard_map/ppermute | solution.py:29
  134.0 27.1 %collective-permute-start.27 = (bf16[384,512]{1,0:T(8,128)(2,1)S(1)}, bf16[384,512]{1,0:T(8,128)(2,1)S(1)}, u32[]{:S(2)}, u32[]{:S(2)}) collective-permute-start(bf16[384,512]{1,0:T(8,128)(2,1)S(1)} %get-tuple-element.134), channel_id=1, source_target_pairs={{0,4},{1,5},{2,6},{3,7},{4,8},{5,9},{6,10},{7,11},{8,12},{9,13},{1... | collective-permute-start | bytes 1179656 | tf_op jit(solution)/shard_map/ppermute | solution.py:29
  135.6 28.3 %collective-permute-start.28 = (bf16[384,512]{1,0:T(8,128)(2,1)S(1)}, bf16[384,512]{1,0:T(8,128)(2,1)S(1)}, u32[]{:S(2)}, u32[]{:S(2)}) collective-permute-start(bf16[384,512]{1,0:T(8,128)(2,1)S(1)} %get-tuple-element.135), channel_id=1, source_target_pairs={{0,12},{1,13},{2,14},{3,15},{4,0},{5,1},{6,2},{7,3},{8,4},{9,5},{1... | collective-permute-start | bytes 1179656 | tf_op jit(solution)/shard_map/ppermute | solution.py:29
  138.4 27.6 %collective-permute-start.38 = (bf16[4,2,64,384]{3,2,1,0:T(8,128)(2,1)S(1)}, bf16[4,2,64,384]{3,2,1,0:T(8,128)(2,1)S(1)}, u32[]{:S(2)}, u32[]{:S(2)}) collective-permute-start(bf16[4,2,64,384]{3,2,1,0:T(8,128)(2,1)S(1)} %stack_far.1.mine), channel_id=1, source_target_pairs={{0,16},{16,0},{32,48},{48,32},{64,80},{80,64},{96,112},{112,96},{1... | collective-permute-start | bytes 1179656 | tf_op jit(solution)/shard_map/ppermute | solution.py:41
where the time goes:
time: 167 us
  waiting for transfers between devices  72 us (43%)
  starting transfers between devices  70.4 us (42%)
  Pallas kernels  18.6 us (11%)
  local copies, waits for them, and re-layouts  4.47 us (3%)
  between operations  1.67 us (1%)
    ppermute x16, waiting for transfers between devices, along_z(): return lax.ppermute(value, 'fsdp', pairs)  59.7 us
    ppermute x16, starting transfers between devices, along_z(): return lax.ppermute(value, 'fsdp', pairs)  36.2 us
    ppermute x15, starting transfers between devices, along_x(): return lax.ppermute(value, 'fsdp', pairs)  28 us
    pallas_call x21, Pallas kernels, kernel_call(): pl.pallas_call(kernel, in_specs=specs, out_specs=[pl.BlockSpec(memory_spa...  12.4 us
    ppermute x15, waiting for transfers between devices, along_x(): return lax.ppermute(value, 'fsdp', pairs)  5.47 us
    ppermute x2, waiting for transfers between devices, swap_far(): return lax.ppermute(value, 'rep', [(r, r ^ 8) for r in range(16)])  4.55 us
    unnamed x30, local copies, waits for them, and re-layouts  4.47 us
    pallas_call x2, Pallas kernels, adam_columns(): pl.pallas_call(kernel, grid=(tiles,), in_specs=[pl.BlockSpec(memory_space...  4.22 us
  transfers between devices with their start and end apart: 39, of which 16 were waited for; matrix products, arithmetic and copies ran while one was open for 0% of the time, Pallas kernels for 10%

commit v1 on v0

--- a/solution.py
+++ b/solution.py
@@ -338,18 +338,18 @@
     )
 
 
-def halve(mine, other, keep, name):
+def halve(mine, other, keep, kind, name):
     shape = (mine.shape[0] // 2, *mine.shape[1:])
 
     def kernel(keep_ref, mine, other, kept, sent):
         for out, which in ((sent, 1 - keep_ref[0]), (kept, keep_ref[0])):
             at = pl.ds(which * shape[0], shape[0])
-            out[...] = mine[at].astype(f32) + other[at].astype(f32)
+            out[...] = (mine[at].astype(f32) + other[at].astype(f32)).astype(out.dtype)
 
     return kernel_call(
         kernel,
         [keep, mine, other],
-        [(shape, f32)] * 2,
+        [(shape, f32), (shape, kind)],
         LIGHT,
         name,
         blocked={0: SMALL},
@@ -474,11 +474,11 @@
         self.state = (mine, swap_core(other))
 
     def reduce_far(self, *since):
-        mine, other = halve(*tie(self.state, *since), self.far, "halve_far")
+        mine, other = halve(*tie(self.state, *since), self.far, bf16, "halve_far")
         self.state = (mine, swap_far(other))
 
     def reduce_near(self, *since):
-        mine, other = halve(*tie(self.state, *since), self.near, "halve_near")
+        mine, other = halve(*tie(self.state, *since), self.near, f32, "halve_near")
         self.state = (mine[0], swap_near(other)[0])
 
     def reduce_pair(self, *since):
@@ -579,7 +579,7 @@
     left, right = along_z(up, 1), along_z(down, -1)
     outer.gather_cores(up)
 
-    own1, one1, far_a, far_b, three1 = partial_grad(turned, tie(resids, up))
+    own1, one1, far_a, far_b, three1 = partial_grad(turned, tie(resids, far_a))
     far_a, far_b = along_z(far_a, 1), along_z(far_b, -1)
     staged = load(tie([shard, moment_first[0], moment_second[0]], own1), "load_state")
 

time: 167 us -> 180 us (1.078)
  the two profiles are of different devices: /device:TPU:16 before, /device:TPU:33 now
where the time goes in v1:
time: 180 us
  starting transfers between devices  81.3 us (45%)
  waiting for transfers between devices  73.3 us (41%)
  Pallas kernels  20.3 us (11%)
  local copies, waits for them, and re-layouts  3.18 us (2%)
    ppermute x16, waiting for transfers between devices, along_z(): return lax.ppermute(value, 'fsdp', pairs)  58.1 us
    ppermute x16, starting transfers between devices, along_z(): return lax.ppermute(value, 'fsdp', pairs)  39.2 us
    ppermute x15, starting transfers between devices, along_x(): return lax.ppermute(value, 'fsdp', pairs)  21.8 us
    pallas_call x21, Pallas kernels, kernel_call(): pl.pallas_call(kernel, in_specs=specs, out_specs=[pl.BlockSpec(memory_spa...  14.1 us
    ppermute x15, waiting for transfers between devices, along_x(): return lax.ppermute(value, 'fsdp', pairs)  13.6 us
    ppermute x2, starting transfers between devices, swap_core(): return lax.ppermute(value, 'rep', [(r, r ^ 1) for r in range(16)])  9.38 us
    ppermute x2, starting transfers between devices, swap_far(): return lax.ppermute(value, 'rep', [(r, r ^ 8) for r in range(16)])  6.15 us
    pallas_call x2, Pallas kernels, adam_columns(): pl.pallas_call(kernel, grid=(tiles,), in_specs=[pl.BlockSpec(memory_space...  4.22 us
  transfers between devices with their start and end apart: 39, of which 14 were waited for; matrix products, arithmetic and copies ran while one was open for 0% of the time, Pallas kernels for 10%

profile of v1, /device:TPU:33, one launch (start us, length us, event | category | flops | bytes accessed | tf_op | source)
XLA Modules:
  0.0 179.8 jit_solution(6478938340443334327)
XLA Ops:
  0.6 1.9 %copy-done = bf16[256,6144]{1,0:T(8,128)(2,1)S(1)} copy-done((bf16[256,6144]{1,0:T(8,128)(2,1)S(1)}, bf16[256,6144]{1,0:T(8,128)(2,1)}, u32[]{:S(2)}) %copy-start) | copy-done | bytes 3145752
  2.5 0.6 pack_tokens.1
  3.2 1.3 collective-permute-start
  4.5 2.4 %collective-permute-start.1 = (bf16[256,1536]{1,0:T(8,128)(2,1)S(1)}, bf16[256,1536]{1,0:T(8,128)(2,1)S(1)}, u32[]{:S(2)}, u32[]{:S(2)}) collective-permute-start(bf16[256,1536]{1,0:T(8,128)(2,1)S(1)} %get-tuple-element.92), channel_id=1, source_target_pairs={{0,2},{1,3},{2,0},{3,1},{4,6},{5,7},{6,4},{7,5},{8,10},{9,11},{10,... | collective-permute-start | bytes 2359304 | tf_op jit(solution)/shard_map/ppermute | solution.py:24
  6.9 1.2 collective-permute-start.2
  8.2 3.1 %collective-permute-start.4 = (bf16[384,512]{1,0:T(8,128)(2,1)S(1)}, bf16[384,512]{1,0:T(8,128)(2,1)S(1)}, u32[]{:S(2)}, u32[]{:S(2)}) collective-permute-start(bf16[384,512]{1,0:T(8,128)(2,1)S(1)} %get-tuple-element.94.refs_4_), channel_id=1, source_target_pairs={{0,4},{1,5},{2,6},{3,7},{4,8},{5,9},{6,10},{7,11},{8,12},{9,13},{1... | collective-permute-start | bytes 1179656 | tf_op jit(solution)/shard_map/ppermute | solution.py:29
  11.2 2.2 %collective-permute-start.3 = (bf16[384,512]{1,0:T(8,128)(2,1)S(1)}, bf16[384,512]{1,0:T(8,128)(2,1)S(1)}, u32[]{:S(2)}, u32[]{:S(2)}) collective-permute-start(bf16[384,512]{1,0:T(8,128)(2,1)S(1)} %get-tuple-element.94.refs_4_), channel_id=1, source_target_pairs={{0,12},{1,13},{2,14},{3,15},{4,0},{5,1},{6,2},{7,3},{8,4},{9,5},{1... | collective-permute-start | bytes 1179656 | tf_op jit(solution)/shard_map/ppermute | solution.py:29
  13.5 17.4 %collective-permute-done.4.previous.refs_8_ = bf16[384,512]{1,0:T(8,128)(2,1)S(1)} collective-permute-done((bf16[384,512]{1,0:T(8,128)(2,1)S(1)}, bf16[384,512]{1,0:T(8,128)(2,1)S(1)}, u32[]{:S(2)}, u32[]{:S(2)}) %collective-permute-start.4) | collective-permute-done | bytes 393248 | tf_op jit(solution)/shard_map/ppermute | solution.py:29
  30.9 0.4 collective-permute-start.5
  31.3 3.2 %collective-permute-start.6 = (bf16[192,512]{1,0:T(8,128)(2,1)S(1)}, bf16[192,512]{1,0:T(8,128)(2,1)S(1)}, u32[]{:S(2)}, u32[]{:S(2)}) collective-permute-start(bf16[192,512]{1,0:T(8,128)(2,1)S(1)} %get-tuple-element.96), channel_id=1, source_target_pairs={{0,12},{1,13},{2,14},{3,15},{4,0},{5,1},{6,2},{7,3},{8,4},{9,5},{1... | collective-permute-start | bytes 589832 | tf_op jit(solution)/shard_map/ppermute | solution.py:29
  34.5 4.0 %collective-permute-done.5.refs_6_ = bf16[192,512]{1,0:T(8,128)(2,1)S(1)} collective-permute-done((bf16[192,512]{1,0:T(8,128)(2,1)S(1)}, bf16[192,512]{1,0:T(8,128)(2,1)S(1)}, u32[]{:S(2)}, u32[]{:S(2)}) %collective-permute-start.5) | collective-permute-done | bytes 196640 | tf_op jit(solution)/shard_map/ppermute | solution.py:29
  38.6 0.7 collective-permute-done.6.refs_7_
  39.3 4.5 %collective-permute-start.7 = (bf16[384,512]{1,0:T(8,128)(2,1)S(1)}, bf16[384,512]{1,0:T(8,128)(2,1)S(1)}, u32[]{:S(2)}, u32[]{:S(2)}) collective-permute-start(bf16[384,512]{1,0:T(8,128)(2,1)S(1)} %get-tuple-element.111.refs_4_), channel_id=1, source_target_pairs={{0,12},{1,13},{2,14},{3,15},{4,0},{5,1},{6,2},{7,3},{8,4},{9,5},{1... | collective-permute-start | bytes 1179656 | tf_op jit(solution)/shard_map/ppermute | solution.py:29
  43.8 2.2 %partial_keys.2 = (f32[256,512]{1,0:T(8,128)S(1)}, bf16[256,512]{1,0:T(8,128)(2,1)S(1)}, bf16[256,512]{1,0:T(8,128)(2,1)}, bf16[256,512]{1,0:T(8,128)(2,1)}) custom-call(bf16[256,1536]{1,0:T(8,128)(2,1)S(1)} %get-tuple-element.98.refs_0_, bf16[256,1536]{1,0:T(8,128)(2,1)S(1)} %collective-permute-done.refs_1_, ...), custom_call_target="tpu_custom_call" | custom-call | flops 40000000000 | bytes 1000000 | tf_op jit(solution)/shard_map/partial_keys/pallas_call | solution.py:57
  46.1 2.1 %collective-permute-start.12 = (bf16[256,512]{1,0:T(8,128)(2,1)}, bf16[256,512]{1,0:T(8,128)(2,1)S(1)}, u32[]{:S(2)}, u32[]{:S(2)}) collective-permute-start(bf16[256,512]{1,0:T(8,128)(2,1)} %get-tuple-element.109), channel_id=1, source_target_pairs={{0,2},{1,3},{2,0},{3,1},{4,6},{5,7},{6,4},{7,5},{8,10},{9,11},{10,... | collective-permute-start | bytes 786440 | tf_op jit(solution)/shard_map/ppermute | solution.py:24
  48.2 2.3 %collective-permute-done.7.following.refs_5_ = bf16[384,512]{1,0:T(8,128)(2,1)S(1)} collective-permute-done((bf16[384,512]{1,0:T(8,128)(2,1)S(1)}, bf16[384,512]{1,0:T(8,128)(2,1)S(1)}, u32[]{:S(2)}, u32[]{:S(2)}) %collective-permute-start.7) | collective-permute-done | bytes 393248 | tf_op jit(solution)/shard_map/ppermute | solution.py:29
  50.5 1.1 collective-permute-done.9.one
  51.6 0.8 outer_halves.3
  52.4 4.7 %collective-permute-start.10 = (bf16[192,512]{1,0:T(8,128)(2,1)}, bf16[192,512]{1,0:T(8,128)(2,1)}, u32[]{:S(2)}, u32[]{:S(2)}) collective-permute-start(bf16[192,512]{1,0:T(8,128)(2,1)} %get-tuple-element.107), channel_id=1, source_target_pairs={{0,4},{1,5},{2,6},{3,7},{4,8},{5,9},{6,10},{7,11},{8,12},{9,13},{1... | collective-permute-start | bytes 589832 | tf_op jit(solution)/shard_map/ppermute | solution.py:29
  57.1 5.5 %collective-permute-start.11 = (bf16[192,512]{1,0:T(8,128)(2,1)}, bf16[192,512]{1,0:T(8,128)(2,1)}, u32[]{:S(2)}, u32[]{:S(2)}) collective-permute-start(bf16[192,512]{1,0:T(8,128)(2,1)} %get-tuple-element.108), channel_id=1, source_target_pairs={{0,12},{1,13},{2,14},{3,15},{4,0},{5,1},{6,2},{7,3},{8,4},{9,5},{1... | collective-permute-start | bytes 589832 | tf_op jit(solution)/shard_map/ppermute | solution.py:29
  62.6 0.3 turn_fragment.1
  62.9 8.1 %collective-permute-start.31 = (bf16[4,2,64,384]{3,2,1,0:T(8,128)(2,1)S(1)}, bf16[4,2,64,384]{3,2,1,0:T(8,128)(2,1)S(1)}, u32[]{:S(2)}, u32[]{:S(2)}) collective-permute-start(bf16[4,2,64,384]{3,2,1,0:T(8,128)(2,1)S(1)} %get-tuple-element.152), channel_id=1, source_target_pairs={{0,16},{16,0},{32,48},{48,32},{64,80},{80,64},{96,112},{112,96},{1... | collective-permute-start | bytes 1179656 | tf_op jit(solution)/shard_map/ppermute | solution.py:41
  71.1 0.2 residual.2.refs_0_
  71.3 1.2 copy-done.13
  72.6 2.8 %partial_keys.3 = (f32[256,512]{1,0:T(8,128)S(1)}, bf16[256,512]{1,0:T(8,128)(2,1)S(1)}, bf16[256,512]{1,0:T(8,128)(2,1)S(1)}, bf16[256,512]{1,0:T(8,128)(2,1)S(1)}) custom-call(bf16[256,1536]{1,0:T(8,128)(2,1)S(1)} %copy-done.7, bf16[256,1536]{1,0:T(8,128)(2,1)S(1)} %copy-done.9, bf16[256,1536]{1,0:T(8,128)(2,1)S(1)} %copy-done.11, ...), custom_call_target="tpu_custom_call" | custom-call | flops 40000000000 | bytes 1000000 | tf_op jit(solution)/shard_map/partial_keys/pallas_call | solution.py:57
  75.4 3.9 %collective-permute-start.14 = (bf16[256,512]{1,0:T(8,128)(2,1)S(1)}, bf16[256,512]{1,0:T(8,128)(2,1)S(1)}, u32[]{:S(2)}, u32[]{:S(2)}) collective-permute-start(bf16[256,512]{1,0:T(8,128)(2,1)S(1)} %get-tuple-element.117), channel_id=1, source_target_pairs={{0,3},{1,0},{2,1},{3,2},{4,7},{5,4},{6,5},{7,6},{8,11},{9,8},{10,9... | collective-permute-start | bytes 786440 | tf_op jit(solution)/shard_map/ppermute | solution.py:24
  79.3 3.0 %collective-permute-start.32 = (bf16[2,2,64,384]{3,2,1,0:T(8,128)(2,1)S(1)}, bf16[2,2,64,384]{3,2,1,0:T(8,128)(2,1)S(1)}, u32[]{:S(2)}, u32[]{:S(2)}) collective-permute-start(bf16[2,2,64,384]{3,2,1,0:T(8,128)(2,1)S(1)} %get-tuple-element.156), channel_id=1, source_target_pairs={{0,128},{16,144},{32,160},{48,176},{64,192},{80,208},{96,224},{112... | collective-permute-start | bytes 589832 | tf_op jit(solution)/shard_map/ppermute | solution.py:37
  83.0 0.2 collective-permute-start.22
  83.3 2.9 %collective-permute-start.21 = (bf16[256,512]{1,0:T(8,128)(2,1)S(1)}, bf16[256,512]{1,0:T(8,128)(2,1)S(1)}, u32[]{:S(2)}, u32[]{:S(2)}) collective-permute-start(bf16[256,512]{1,0:T(8,128)(2,1)S(1)} %residual.2.refs_0_), channel_id=1, source_target_pairs={{0,2},{1,3},{2,0},{3,1},{4,6},{5,7},{6,4},{7,5},{8,10},{9,11},{10,... | collective-permute-start | bytes 786440 | tf_op jit(solution)/shard_map/ppermute | solution.py:24
  86.2 0.8 collective-permute-start.20
  87.0 0.6 collective-permute-done.14.one
  87.6 0.6 collective-permute-start.16
  88.2 1.3 collective-permute-start.33
  89.5 0.9 transpose_tokens.1.turned_ref
  90.5 11.8 %collective-permute-done.16.three = bf16[256,512]{1,0:T(8,128)(2,1)S(1)} collective-permute-done((bf16[256,512]{1,0:T(8,128)(2,1)S(1)}, bf16[256,512]{1,0:T(8,128)(2,1)S(1)}, u32[]{:S(2)}, u32[]{:S(2)}) %collective-permute-start.16) | collective-permute-done | bytes 262176 | tf_op jit(solution)/shard_map/ppermute | solution.py:24
  102.3 0.2 residual.3.refs_0_
  102.6 5.5 %collective-permute-start.18 = (bf16[256,512]{1,0:T(8,128)(2,1)S(1)}, bf16[256,512]{1,0:T(8,128)(2,1)S(1)}, u32[]{:S(2)}, u32[]{:S(2)}) collective-permute-start(bf16[256,512]{1,0:T(8,128)(2,1)S(1)} %residual.3.refs_0_), channel_id=1, source_target_pairs={{0,2},{1,3},{2,0},{3,1},{4,6},{5,7},{6,4},{7,5},{8,10},{9,11},{10,... | collective-permute-start | bytes 786440 | tf_op jit(solution)/shard_map/ppermute | solution.py:24
  108.1 0.8 collective-permute-start.17
  108.9 1.5 collective-permute-start.34
  110.4 1.8 partial_grad.2
  112.2 1.6 collective-permute-done.34.other
  113.7 2.9 %collective-permute-start.23 = (bf16[192,512]{1,0:T(8,128)(2,1)S(1)}, bf16[192,512]{1,0:T(8,128)(2,1)S(1)}, u32[]{:S(2)}, u32[]{:S(2)}) collective-permute-start(bf16[192,512]{1,0:T(8,128)(2,1)S(1)} %get-tuple-element.120), channel_id=1, source_target_pairs={{0,4},{1,5},{2,6},{3,7},{4,8},{5,9},{6,10},{7,11},{8,12},{9,13},{1... | collective-permute-start | bytes 589832 | tf_op jit(solution)/shard_map/ppermute | solution.py:29
  116.6 2.9 %collective-permute-start.28 = (bf16[192,512]{1,0:T(8,128)(2,1)S(1)}, bf16[192,512]{1,0:T(8,128)(2,1)S(1)}, u32[]{:S(2)}, u32[]{:S(2)}) collective-permute-start(bf16[192,512]{1,0:T(8,128)(2,1)S(1)} %get-tuple-element.141), channel_id=1, source_target_pairs={{0,12},{1,13},{2,14},{3,15},{4,0},{5,1},{6,2},{7,3},{8,4},{9,5},{1... | collective-permute-start | bytes 589832 | tf_op jit(solution)/shard_map/ppermute | solution.py:29
  119.5 0.8 nesterov.1
  120.3 8.0 %collective-permute-done.23.far_a = bf16[192,512]{1,0:T(8,128)(2,1)S(1)} collective-permute-done((bf16[192,512]{1,0:T(8,128)(2,1)S(1)}, bf16[192,512]{1,0:T(8,128)(2,1)S(1)}, u32[]{:S(2)}, u32[]{:S(2)}) %collective-permute-start.23) | collective-permute-done | bytes 196640 | tf_op jit(solution)/shard_map/ppermute | solution.py:29
  128.4 1.9 %collective-permute-start.36 = (bf16[1,2,64,384]{3,2,1,0:T(8,128)(2,1)S(1)}, bf16[1,2,64,384]{3,2,1,0:T(8,128)(2,1)S(1)}, u32[]{:S(2)}, u32[]{:S(2)}) collective-permute-start(bf16[1,2,64,384]{3,2,1,0:T(8,128)(2,1)S(1)} %bitcast.26), channel_id=1, source_target_pairs={{0,64},{16,80},{32,96},{48,112},{64,0},{80,16},{96,32},{112,48},{1... | collective-permute-start | bytes 294920 | tf_op jit(solution)/shard_map/ppermute | solution.py:33
  130.3 1.8 partial_grad.3
  132.2 3.6 %collective-permute-start.25 = (bf16[192,512]{1,0:T(8,128)(2,1)S(1)}, bf16[192,512]{1,0:T(8,128)(2,1)S(1)}, u32[]{:S(2)}, u32[]{:S(2)}) collective-permute-start(bf16[192,512]{1,0:T(8,128)(2,1)S(1)} %get-tuple-element.129), channel_id=1, source_target_pairs={{0,12},{1,13},{2,14},{3,15},{4,0},{5,1},{6,2},{7,3},{8,4},{9,5},{1... | collective-permute-start | bytes 589832 | tf_op jit(solution)/shard_map/ppermute | solution.py:29
  135.8 3.1 %collective-permute-start.37 = (bf16[2,2,64,384]{3,2,1,0:T(8,128)(2,1)S(1)}, bf16[2,2,64,384]{3,2,1,0:T(8,128)(2,1)S(1)}, u32[]{:S(2)}, u32[]{:S(2)}) collective-permute-start(bf16[2,2,64,384]{3,2,1,0:T(8,128)(2,1)S(1)} %stack_near.1.mine), channel_id=1, source_target_pairs={{0,128},{16,144},{32,160},{48,176},{64,192},{80,208},{96,224},{112... | collective-permute-start | bytes 589832 | tf_op jit(solution)/shard_map/ppermute | solution.py:37
  138.9 0.1 add_halves.3
  139.0 1.2 collective-permute-start.30
  140.3 1.2 collective-permute-start.29
  141.5 0.9 collective-permute-done.24.far_a
  142.3 17.3 %collective-permute-done.25.far_b = bf16[192,512]{1,0:T(8,128)(2,1)S(1)} collective-permute-done((bf16[192,512]{1,0:T(8,128)(2,1)S(1)}, bf16[192,512]{1,0:T(8,128)(2,1)S(1)}, u32[]{:S(2)}, u32[]{:S(2)}) %collective-permute-start.25) | collective-permute-done | bytes 196640 | tf_op jit(solution)/shard_map/ppermute | solution.py:29
  159.6 0.1 add_halves.2
  159.8 3.6 %collective-permute-start.27 = (bf16[384,512]{1,0:T(8,128)(2,1)S(1)}, bf16[384,512]{1,0:T(8,128)(2,1)S(1)}, u32[]{:S(2)}, u32[]{:S(2)}) collective-permute-start(bf16[384,512]{1,0:T(8,128)(2,1)S(1)} %get-tuple-element.131), channel_id=1, source_target_pairs={{0,12},{1,13},{2,14},{3,15},{4,0},{5,1},{6,2},{7,3},{8,4},{9,5},{1... | collective-permute-start | bytes 1179656 | tf_op jit(solution)/shard_map/ppermute | solution.py:29
  163.4 1.2 collective-permute-start.38
  164.7 2.2 %load_state.1 = (bf16[384,1024]{1,0:T(8,128)(2,1)S(1)}, f32[384,1024]{1,0:T(8,128)S(1)}, f32[384,1024]{1,0:T(8,128)S(1)}) custom-call(bf16[384,1024]{1,0:T(8,128)(2,1)} %bitcast.17, f32[384,1024]{1,0:T(8,128)} %bitcast.30, f32[384,1024]{1,0:T(8,128)} %bitcast.31), custom_call_target="tpu_custom_call" | custom-call | flops 1 | bytes 1 | tf_op jit(solution)/shard_map/load_state/pallas_call | solution.py:57
  166.8 1.2 collective-permute-done.30.right
  168.1 2.1 %adam_columns.2 = (bf16[384,1024]{1,0:T(8,128)(2,1)}, f32[384,1024]{1,0:T(8,128)}, f32[384,1024]{1,0:T(8,128)}) custom-call(f32[384,512]{1,0:T(8,128)S(1)} %get-tuple-element.138.own, bf16[384,512]{1,0:T(8,128)(2,1)S(1)} %collective-permute-done.29.left, bf16[384,512]{1,0:T(8,128)(2,1)S(1)} %collective-permute-done.30.right, ...), custom_call_target="tpu_custom_call" | custom-call | flops 1 | bytes 1 | tf_op jit(solution)/shard_map/adam_columns/pallas_call | solution.py:300
  170.2 6.1 %collective-permute-done.26.left = bf16[384,512]{1,0:T(8,128)(2,1)S(1)} collective-permute-done((bf16[384,512]{1,0:T(8,128)(2,1)S(1)}, bf16[384,512]{1,0:T(8,128)(2,1)S(1)}, u32[]{:S(2)}, u32[]{:S(2)}) %collective-permute-start.26) | collective-permute-done | bytes 393248 | tf_op jit(solution)/shard_map/ppermute | solution.py:29
  176.3 0.2 collective-permute-done.27.right
  176.5 2.1 %adam_columns.3 = (bf16[384,1024]{1,0:T(8,128)(2,1)}, f32[384,1024]{1,0:T(8,128)}, f32[384,1024]{1,0:T(8,128)}) custom-call(f32[384,512]{1,0:T(8,128)S(1)} %get-tuple-element.125.own, bf16[384,512]{1,0:T(8,128)(2,1)S(1)} %collective-permute-done.26.left, ...), custom_call_target="tpu_custom_call", output_to_operand_aliasing={{0}: (6, {}), {1}: (7, {}), {2}: (8, {})} | custom-call | flops 1 | bytes 1 | tf_op jit(solution)/shard_map/adam_columns/pallas_call | solution.py:300
  178.6 1.2 weave.1
  (71 shorter events, 0.8 us)
Async XLA Ops:
  0.6 1.9 %copy-start = (bf16[256,6144]{1,0:T(8,128)(2,1)S(1)}, bf16[256,6144]{1,0:T(8,128)(2,1)}, u32[]{:S(2)}) copy-start(bf16[256,6144]{1,0:T(8,128)(2,1)} %source.1) | copy-start | bytes 9437188
  2.5 5.5 %copy-start.1 = (bf16[1,384,1024]{2,1,0:T(8,128)(2,1)S(1)}, bf16[1,384,1024]{2,1,0:T(8,128)(2,1)}, u32[]{:S(2)}) copy-start(bf16[1,384,1024]{2,1,0:T(8,128)(2,1)} %param.11) | copy-start | bytes 2359300
  3.2 42.8 %copy-start.6 = (bf16[256,1536]{1,0:T(8,128)(2,1)}, bf16[256,1536]{1,0:T(8,128)(2,1)S(1)}, u32[]{:S(2)}) copy-start(bf16[256,1536]{1,0:T(8,128)(2,1)S(1)} %get-tuple-element.98.refs_0_) | copy-start | bytes 2359300
  3.2 40.6 %collective-permute-start = (bf16[256,1536]{1,0:T(8,128)(2,1)S(1)}, bf16[256,1536]{1,0:T(8,128)(2,1)S(1)}, u32[]{:S(2)}, u32[]{:S(2)}) collective-permute-start(bf16[256,1536]{1,0:T(8,128)(2,1)S(1)} %get-tuple-element.91), channel_id=1, source_target_pairs={{0,1},{1,2},{2,3},{3,0},{4,5},{5,6},{6,7},{7,4},{8,9},{9,10},{10,1... | collective-permute-start | bytes 2359304 | tf_op jit(solution)/shard_map/ppermute | solution.py:24
  4.5 39.3 %collective-permute-start.1 = (bf16[256,1536]{1,0:T(8,128)(2,1)S(1)}, bf16[256,1536]{1,0:T(8,128)(2,1)S(1)}, u32[]{:S(2)}, u32[]{:S(2)}) collective-permute-start(bf16[256,1536]{1,0:T(8,128)(2,1)S(1)} %get-tuple-element.92), channel_id=1, source_target_pairs={{0,2},{1,3},{2,0},{3,1},{4,6},{5,7},{6,4},{7,5},{8,10},{9,11},{10,... | collective-permute-start | bytes 2359304 | tf_op jit(solution)/shard_map/ppermute | solution.py:24
  6.9 36.8 %collective-permute-start.2 = (bf16[256,1536]{1,0:T(8,128)(2,1)S(1)}, bf16[256,1536]{1,0:T(8,128)(2,1)S(1)}, u32[]{:S(2)}, u32[]{:S(2)}) collective-permute-start(bf16[256,1536]{1,0:T(8,128)(2,1)S(1)} %get-tuple-element.93), channel_id=1, source_target_pairs={{0,3},{1,0},{2,1},{3,2},{4,7},{5,4},{6,5},{7,6},{8,11},{9,8},{10,9... | collective-permute-start | bytes 2359304 | tf_op jit(solution)/shard_map/ppermute | solution.py:24
  8.2 37.8 %copy-start.14 = (bf16[384,512]{1,0:T(8,128)(2,1)}, bf16[384,512]{1,0:T(8,128)(2,1)S(1)}, u32[]{:S(2)}) copy-start(bf16[384,512]{1,0:T(8,128)(2,1)S(1)} %get-tuple-element.111.refs_4_) | copy-start | bytes 1179652
  8.2 22.7 %collective-permute-start.4 = (bf16[384,512]{1,0:T(8,128)(2,1)S(1)}, bf16[384,512]{1,0:T(8,128)(2,1)S(1)}, u32[]{:S(2)}, u32[]{:S(2)}) collective-permute-start(bf16[384,512]{1,0:T(8,128)(2,1)S(1)} %get-tuple-element.94.refs_4_), channel_id=1, source_target_pairs={{0,4},{1,5},{2,6},{3,7},{4,8},{5,9},{6,10},{7,11},{8,12},{9,13},{1... | collective-permute-start | bytes 1179656 | tf_op jit(solution)/shard_map/ppermute | solution.py:29
  11.2 19.6 %collective-permute-start.3 = (bf16[384,512]{1,0:T(8,128)(2,1)S(1)}, bf16[384,512]{1,0:T(8,128)(2,1)S(1)}, u32[]{:S(2)}, u32[]{:S(2)}) collective-permute-start(bf16[384,512]{1,0:T(8,128)(2,1)S(1)} %get-tuple-element.94.refs_4_), channel_id=1, source_target_pairs={{0,12},{1,13},{2,14},{3,15},{4,0},{5,1},{6,2},{7,3},{8,4},{9,5},{1... | collective-permute-start | bytes 1179656 | tf_op jit(solution)/shard_map/ppermute | solution.py:29
  30.9 7.7 %collective-permute-start.5 = (bf16[192,512]{1,0:T(8,128)(2,1)S(1)}, bf16[192,512]{1,0:T(8,128)(2,1)S(1)}, u32[]{:S(2)}, u32[]{:S(2)}) collective-permute-start(bf16[192,512]{1,0:T(8,128)(2,1)S(1)} %get-tuple-element.95), channel_id=1, source_target_pairs={{0,4},{1,5},{2,6},{3,7},{4,8},{5,9},{6,10},{7,11},{8,12},{9,13},{1... | collective-permute-start | bytes 589832 | tf_op jit(solution)/shard_map/ppermute | solution.py:29
  31.3 8.0 %collective-permute-start.6 = (bf16[192,512]{1,0:T(8,128)(2,1)S(1)}, bf16[192,512]{1,0:T(8,128)(2,1)S(1)}, u32[]{:S(2)}, u32[]{:S(2)}) collective-permute-start(bf16[192,512]{1,0:T(8,128)(2,1)S(1)} %get-tuple-element.96), channel_id=1, source_target_pairs={{0,12},{1,13},{2,14},{3,15},{4,0},{5,1},{6,2},{7,3},{8,4},{9,5},{1... | collective-permute-start | bytes 589832 | tf_op jit(solution)/shard_map/ppermute | solution.py:29
  38.6 9.6 %collective-permute-start.8 = (bf16[384,512]{1,0:T(8,128)(2,1)S(1)}, bf16[384,512]{1,0:T(8,128)(2,1)S(1)}, u32[]{:S(2)}, u32[]{:S(2)}) collective-permute-start(bf16[384,512]{1,0:T(8,128)(2,1)S(1)} %get-tuple-element.111.refs_4_), channel_id=1, source_target_pairs={{0,4},{1,5},{2,6},{3,7},{4,8},{5,9},{6,10},{7,11},{8,12},{9,13},{1... | collective-permute-start | bytes 1179656 | tf_op jit(solution)/shard_map/ppermute | solution.py:29
  39.3 11.3 %collective-permute-start.7 = (bf16[384,512]{1,0:T(8,128)(2,1)S(1)}, bf16[384,512]{1,0:T(8,128)(2,1)S(1)}, u32[]{:S(2)}, u32[]{:S(2)}) collective-permute-start(bf16[384,512]{1,0:T(8,128)(2,1)S(1)} %get-tuple-element.111.refs_4_), channel_id=1, source_target_pairs={{0,12},{1,13},{2,14},{3,15},{4,0},{5,1},{6,2},{7,3},{8,4},{9,5},{1... | collective-permute-start | bytes 1179656 | tf_op jit(solution)/shard_map/ppermute | solution.py:29
  43.7 2.2 %copy-start.8 = (bf16[256,1536]{1,0:T(8,128)(2,1)}, bf16[256,1536]{1,0:T(8,128)(2,1)S(1)}, u32[]{:S(2)}) copy-start(bf16[256,1536]{1,0:T(8,128)(2,1)S(1)} %collective-permute-done.refs_1_) | copy-start | bytes 2359300
  43.7 2.2 %copy-start.10 = (bf16[256,1536]{1,0:T(8,128)(2,1)}, bf16[256,1536]{1,0:T(8,128)(2,1)S(1)}, u32[]{:S(2)}) copy-start(bf16[256,1536]{1,0:T(8,128)(2,1)S(1)} %collective-permute-done.1.refs_2_) | copy-start | bytes 2359300
  43.8 2.2 %copy-start.12 = (bf16[256,1536]{1,0:T(8,128)(2,1)}, bf16[256,1536]{1,0:T(8,128)(2,1)S(1)}, u32[]{:S(2)}) copy-start(bf16[256,1536]{1,0:T(8,128)(2,1)S(1)} %collective-permute-done.2.refs_3_) | copy-start | bytes 2359300
  43.8 18.9 %copy-start.3 = (bf16[1,384,1024]{2,1,0:T(8,128)(2,1)S(1)}, bf16[1,384,1024]{2,1,0:T(8,128)(2,1)}, u32[]{:S(2)}) copy-start(bf16[1,384,1024]{2,1,0:T(8,128)(2,1)} %param.14) | copy-start | bytes 2359300
  46.0 25.1 %copy-start.2 = (bf16[256,1024]{1,0:T(8,128)(2,1)S(1)}, bf16[256,1024]{1,0:T(8,128)(2,1)}, u32[]{:S(2)}) copy-start(bf16[256,1024]{1,0:T(8,128)(2,1)} %goals.3) | copy-start | bytes 1572868
  46.0 5.6 %collective-permute-start.9 = (bf16[256,512]{1,0:T(8,128)(2,1)S(1)}, bf16[256,512]{1,0:T(8,128)(2,1)S(1)}, u32[]{:S(2)}, u32[]{:S(2)}) collective-permute-start(bf16[256,512]{1,0:T(8,128)(2,1)S(1)} %get-tuple-element.103), channel_id=1, source_target_pairs={{0,3},{1,0},{2,1},{3,2},{4,7},{5,4},{6,5},{7,6},{8,11},{9,8},{10,9... | collective-permute-start | bytes 786440 | tf_op jit(solution)/shard_map/ppermute | solution.py:24
  46.1 24.9 %collective-permute-start.12 = (bf16[256,512]{1,0:T(8,128)(2,1)}, bf16[256,512]{1,0:T(8,128)(2,1)S(1)}, u32[]{:S(2)}, u32[]{:S(2)}) collective-permute-start(bf16[256,512]{1,0:T(8,128)(2,1)} %get-tuple-element.109), channel_id=1, source_target_pairs={{0,2},{1,3},{2,0},{3,1},{4,6},{5,7},{6,4},{7,5},{8,10},{9,11},{10,... | collective-permute-start | bytes 786440 | tf_op jit(solution)/shard_map/ppermute | solution.py:24
  48.2 22.9 %collective-permute-start.13 = (bf16[256,512]{1,0:T(8,128)(2,1)}, bf16[256,512]{1,0:T(8,128)(2,1)S(1)}, u32[]{:S(2)}, u32[]{:S(2)}) collective-permute-start(bf16[256,512]{1,0:T(8,128)(2,1)} %get-tuple-element.110), channel_id=1, source_target_pairs={{0,1},{1,2},{2,3},{3,0},{4,5},{5,6},{6,7},{7,4},{8,9},{9,10},{10,1... | collective-permute-start | bytes 786440 | tf_op jit(solution)/shard_map/ppermute | solution.py:24
  52.4 18.9 %collective-permute-start.10 = (bf16[192,512]{1,0:T(8,128)(2,1)}, bf16[192,512]{1,0:T(8,128)(2,1)}, u32[]{:S(2)}, u32[]{:S(2)}) collective-permute-start(bf16[192,512]{1,0:T(8,128)(2,1)} %get-tuple-element.107), channel_id=1, source_target_pairs={{0,4},{1,5},{2,6},{3,7},{4,8},{5,9},{6,10},{7,11},{8,12},{9,13},{1... | collective-permute-start | bytes 589832 | tf_op jit(solution)/shard_map/ppermute | solution.py:29
  57.1 14.2 %collective-permute-start.11 = (bf16[192,512]{1,0:T(8,128)(2,1)}, bf16[192,512]{1,0:T(8,128)(2,1)}, u32[]{:S(2)}, u32[]{:S(2)}) collective-permute-start(bf16[192,512]{1,0:T(8,128)(2,1)} %get-tuple-element.108), channel_id=1, source_target_pairs={{0,12},{1,13},{2,14},{3,15},{4,0},{5,1},{6,2},{7,3},{8,4},{9,5},{1... | collective-permute-start | bytes 589832 | tf_op jit(solution)/shard_map/ppermute | solution.py:29
  62.6 8.7 %copy-start.7 = (bf16[256,1536]{1,0:T(8,128)(2,1)S(1)}, bf16[256,1536]{1,0:T(8,128)(2,1)}, u32[]{:S(2)}) copy-start(bf16[256,1536]{1,0:T(8,128)(2,1)} %copy-done.6) | copy-start | bytes 2359300
  62.6 8.7 %copy-start.9 = (bf16[256,1536]{1,0:T(8,128)(2,1)S(1)}, bf16[256,1536]{1,0:T(8,128)(2,1)}, u32[]{:S(2)}) copy-start(bf16[256,1536]{1,0:T(8,128)(2,1)} %copy-done.8) | copy-start | bytes 2359300
  62.6 8.7 %copy-start.11 = (bf16[256,1536]{1,0:T(8,128)(2,1)S(1)}, bf16[256,1536]{1,0:T(8,128)(2,1)}, u32[]{:S(2)}) copy-start(bf16[256,1536]{1,0:T(8,128)(2,1)} %copy-done.10) | copy-start | bytes 2359300
  62.6 8.7 %copy-start.15 = (bf16[384,512]{1,0:T(8,128)(2,1)S(1)}, bf16[384,512]{1,0:T(8,128)(2,1)}, u32[]{:S(2)}) copy-start(bf16[384,512]{1,0:T(8,128)(2,1)} %copy-done.14) | copy-start | bytes 1179652
  62.9 16.3 %collective-permute-start.31 = (bf16[4,2,64,384]{3,2,1,0:T(8,128)(2,1)S(1)}, bf16[4,2,64,384]{3,2,1,0:T(8,128)(2,1)S(1)}, u32[]{:S(2)}, u32[]{:S(2)}) collective-permute-start(bf16[4,2,64,384]{3,2,1,0:T(8,128)(2,1)S(1)} %get-tuple-element.152), channel_id=1, source_target_pairs={{0,16},{16,0},{32,48},{48,32},{64,80},{80,64},{96,112},{112,96},{1... | collective-permute-start | bytes 1179656 | tf_op jit(solution)/shard_map/ppermute | solution.py:41
  71.2 11.8 %copy-start.4 = (f32[2,384,64]{1,2,0:T(8,128)S(1)}, f32[2,384,64]{1,2,0:T(8,128)}, u32[]{:S(2)}) copy-start(f32[2,384,64]{1,2,0:T(8,128)} %param.15) | copy-start | bytes 589828
  71.2 11.8 %copy-start.5 = (f32[2,384,64]{1,2,0:T(8,128)S(1)}, f32[2,384,64]{1,2,0:T(8,128)}, u32[]{:S(2)}) copy-start(f32[2,384,64]{1,2,0:T(8,128)} %param.16) | copy-start | bytes 589828
  71.3 1.2 copy-start.13
  75.4 12.2 %collective-permute-start.14 = (bf16[256,512]{1,0:T(8,128)(2,1)S(1)}, bf16[256,512]{1,0:T(8,128)(2,1)S(1)}, u32[]{:S(2)}, u32[]{:S(2)}) collective-permute-start(bf16[256,512]{1,0:T(8,128)(2,1)S(1)} %get-tuple-element.117), channel_id=1, source_target_pairs={{0,3},{1,0},{2,1},{3,2},{4,7},{5,4},{6,5},{7,6},{8,11},{9,8},{10,9... | collective-permute-start | bytes 786440 | tf_op jit(solution)/shard_map/ppermute | solution.py:24
  79.2 9.0 %collective-permute-start.15 = (bf16[256,512]{1,0:T(8,128)(2,1)S(1)}, bf16[256,512]{1,0:T(8,128)(2,1)S(1)}, u32[]{:S(2)}, u32[]{:S(2)}) collective-permute-start(bf16[256,512]{1,0:T(8,128)(2,1)S(1)} %get-tuple-element.118), channel_id=1, source_target_pairs={{0,2},{1,3},{2,0},{3,1},{4,6},{5,7},{6,4},{7,5},{8,10},{9,11},{10,... | collective-permute-start | bytes 786440 | tf_op jit(solution)/shard_map/ppermute | solution.py:24
  79.3 6.9 %collective-permute-start.32 = (bf16[2,2,64,384]{3,2,1,0:T(8,128)(2,1)S(1)}, bf16[2,2,64,384]{3,2,1,0:T(8,128)(2,1)S(1)}, u32[]{:S(2)}, u32[]{:S(2)}) collective-permute-start(bf16[2,2,64,384]{3,2,1,0:T(8,128)(2,1)S(1)} %get-tuple-element.156), channel_id=1, source_target_pairs={{0,128},{16,144},{32,160},{48,176},{64,192},{80,208},{96,224},{112... | collective-permute-start | bytes 589832 | tf_op jit(solution)/shard_map/ppermute | solution.py:37
  83.0 19.5 %collective-permute-start.22 = (bf16[256,512]{1,0:T(8,128)(2,1)S(1)}, bf16[256,512]{1,0:T(8,128)(2,1)S(1)}, u32[]{:S(2)}, u32[]{:S(2)}) collective-permute-start(bf16[256,512]{1,0:T(8,128)(2,1)S(1)} %residual.2.refs_0_), channel_id=1, source_target_pairs={{0,3},{1,0},{2,1},{3,2},{4,7},{5,4},{6,5},{7,6},{8,11},{9,8},{10,9... | collective-permute-start | bytes 786440 | tf_op jit(solution)/shard_map/ppermute | solution.py:24
  83.3 24.8 %collective-permute-start.21 = (bf16[256,512]{1,0:T(8,128)(2,1)S(1)}, bf16[256,512]{1,0:T(8,128)(2,1)S(1)}, u32[]{:S(2)}, u32[]{:S(2)}) collective-permute-start(bf16[256,512]{1,0:T(8,128)(2,1)S(1)} %residual.2.refs_0_), channel_id=1, source_target_pairs={{0,2},{1,3},{2,0},{3,1},{4,6},{5,7},{6,4},{7,5},{8,10},{9,11},{10,... | collective-permute-start | bytes 786440 | tf_op jit(solution)/shard_map/ppermute | solution.py:24
  86.2 22.7 %collective-permute-start.20 = (bf16[256,512]{1,0:T(8,128)(2,1)S(1)}, bf16[256,512]{1,0:T(8,128)(2,1)S(1)}, u32[]{:S(2)}, u32[]{:S(2)}) collective-permute-start(bf16[256,512]{1,0:T(8,128)(2,1)S(1)} %residual.2.refs_0_), channel_id=1, source_target_pairs={{0,1},{1,2},{2,3},{3,0},{4,5},{5,6},{6,7},{7,4},{8,9},{9,10},{10,1... | collective-permute-start | bytes 786440 | tf_op jit(solution)/shard_map/ppermute | solution.py:24
  87.6 14.7 %collective-permute-start.16 = (bf16[256,512]{1,0:T(8,128)(2,1)S(1)}, bf16[256,512]{1,0:T(8,128)(2,1)S(1)}, u32[]{:S(2)}, u32[]{:S(2)}) collective-permute-start(bf16[256,512]{1,0:T(8,128)(2,1)S(1)} %get-tuple-element.119), channel_id=1, source_target_pairs={{0,1},{1,2},{2,3},{3,0},{4,5},{5,6},{6,7},{7,4},{8,9},{9,10},{10,1... | collective-permute-start | bytes 786440 | tf_op jit(solution)/shard_map/ppermute | solution.py:24
  88.2 14.2 %collective-permute-start.33 = (f32[1,2,64,384]{3,2,1,0:T(8,128)S(1)}, f32[1,2,64,384]{3,2,1,0:T(8,128)S(1)}, u32[]{:S(2)}, u32[]{:S(2)}) collective-permute-start(f32[1,2,64,384]{3,2,1,0:T(8,128)S(1)} %get-tuple-element.160), channel_id=1, source_target_pairs={{0,64},{16,80},{32,96},{48,112},{64,0},{80,16},{96,32},{112,48},{1... | collective-permute-start | bytes 589832 | tf_op jit(solution)/shard_map/ppermute | solution.py:33
  102.3 14.3 %collective-permute-start.35 = (f32[2,64,384]{2,1,0:T(8,128)S(1)}, f32[2,64,384]{2,1,0:T(8,128)S(1)}, u32[]{:S(2)}, u32[]{:S(2)}) collective-permute-start(f32[2,64,384]{2,1,0:T(8,128)S(1)} %chosen_params.1.own), channel_id=1, source_target_pairs={{0,32},{16,48},{32,0},{48,16},{64,96},{80,112},{96,64},{112,80},{1... | collective-permute-start | bytes 589832 | tf_op jit(solution)/shard_map/ppermute | solution.py:45
  102.5 27.8 %collective-permute-start.19 = (bf16[256,512]{1,0:T(8,128)(2,1)S(1)}, bf16[256,512]{1,0:T(8,128)(2,1)S(1)}, u32[]{:S(2)}, u32[]{:S(2)}) collective-permute-start(bf16[256,512]{1,0:T(8,128)(2,1)S(1)} %residual.3.refs_0_), channel_id=1, source_target_pairs={{0,3},{1,0},{2,1},{3,2},{4,7},{5,4},{6,5},{7,6},{8,11},{9,8},{10,9... | collective-permute-start | bytes 786440 | tf_op jit(solution)/shard_map/ppermute | solution.py:24
  102.6 27.7 %collective-permute-start.18 = (bf16[256,512]{1,0:T(8,128)(2,1)S(1)}, bf16[256,512]{1,0:T(8,128)(2,1)S(1)}, u32[]{:S(2)}, u32[]{:S(2)}) collective-permute-start(bf16[256,512]{1,0:T(8,128)(2,1)S(1)} %residual.3.refs_0_), channel_id=1, source_target_pairs={{0,2},{1,3},{2,0},{3,1},{4,6},{5,7},{6,4},{7,5},{8,10},{9,11},{10,... | collective-permute-start | bytes 786440 | tf_op jit(solution)/shard_map/ppermute | solution.py:24
  108.1 22.2 %collective-permute-start.17 = (bf16[256,512]{1,0:T(8,128)(2,1)S(1)}, bf16[256,512]{1,0:T(8,128)(2,1)S(1)}, u32[]{:S(2)}, u32[]{:S(2)}) collective-permute-start(bf16[256,512]{1,0:T(8,128)(2,1)S(1)} %residual.3.refs_0_), channel_id=1, source_target_pairs={{0,1},{1,2},{2,3},{3,0},{4,5},{5,6},{6,7},{7,4},{8,9},{9,10},{10,1... | collective-permute-start | bytes 786440 | tf_op jit(solution)/shard_map/ppermute | solution.py:24
  108.9 4.8 %collective-permute-start.34 = (f32[2,64,384]{2,1,0:T(8,128)S(1)}, f32[2,64,384]{2,1,0:T(8,128)S(1)}, u32[]{:S(2)}, u32[]{:S(2)}) collective-permute-start(f32[2,64,384]{2,1,0:T(8,128)S(1)} %total.1.mine), channel_id=1, source_target_pairs={{0,32},{16,48},{32,0},{48,16},{64,96},{80,112},{96,64},{112,80},{1... | collective-permute-start | bytes 589832 | tf_op jit(solution)/shard_map/ppermute | solution.py:45
  113.7 14.6 %collective-permute-start.23 = (bf16[192,512]{1,0:T(8,128)(2,1)S(1)}, bf16[192,512]{1,0:T(8,128)(2,1)S(1)}, u32[]{:S(2)}, u32[]{:S(2)}) collective-permute-start(bf16[192,512]{1,0:T(8,128)(2,1)S(1)} %get-tuple-element.120), channel_id=1, source_target_pairs={{0,4},{1,5},{2,6},{3,7},{4,8},{5,9},{6,10},{7,11},{8,12},{9,13},{1... | collective-permute-start | bytes 589832 | tf_op jit(solution)/shard_map/ppermute | solution.py:29
  116.6 22.3 %collective-permute-start.28 = (bf16[192,512]{1,0:T(8,128)(2,1)S(1)}, bf16[192,512]{1,0:T(8,128)(2,1)S(1)}, u32[]{:S(2)}, u32[]{:S(2)}) collective-permute-start(bf16[192,512]{1,0:T(8,128)(2,1)S(1)} %get-tuple-element.141), channel_id=1, source_target_pairs={{0,12},{1,13},{2,14},{3,15},{4,0},{5,1},{6,2},{7,3},{8,4},{9,5},{1... | collective-permute-start | bytes 589832 | tf_op jit(solution)/shard_map/ppermute | solution.py:29
  128.4 7.4 %collective-permute-start.36 = (bf16[1,2,64,384]{3,2,1,0:T(8,128)(2,1)S(1)}, bf16[1,2,64,384]{3,2,1,0:T(8,128)(2,1)S(1)}, u32[]{:S(2)}, u32[]{:S(2)}) collective-permute-start(bf16[1,2,64,384]{3,2,1,0:T(8,128)(2,1)S(1)} %bitcast.26), channel_id=1, source_target_pairs={{0,64},{16,80},{32,96},{48,112},{64,0},{80,16},{96,32},{112,48},{1... | collective-permute-start | bytes 294920 | tf_op jit(solution)/shard_map/ppermute | solution.py:33
  132.1 10.2 %collective-permute-start.24 = (bf16[192,512]{1,0:T(8,128)(2,1)S(1)}, bf16[192,512]{1,0:T(8,128)(2,1)S(1)}, u32[]{:S(2)}, u32[]{:S(2)}) collective-permute-start(bf16[192,512]{1,0:T(8,128)(2,1)S(1)} %get-tuple-element.127), channel_id=1, source_target_pairs={{0,4},{1,5},{2,6},{3,7},{4,8},{5,9},{6,10},{7,11},{8,12},{9,13},{1... | collective-permute-start | bytes 589832 | tf_op jit(solution)/shard_map/ppermute | solution.py:29
  132.2 27.4 %collective-permute-start.25 = (bf16[192,512]{1,0:T(8,128)(2,1)S(1)}, bf16[192,512]{1,0:T(8,128)(2,1)S(1)}, u32[]{:S(2)}, u32[]{:S(2)}) collective-permute-start(bf16[192,512]{1,0:T(8,128)(2,1)S(1)} %get-tuple-element.129), channel_id=1, source_target_pairs={{0,12},{1,13},{2,14},{3,15},{4,0},{5,1},{6,2},{7,3},{8,4},{9,5},{1... | collective-permute-start | bytes 589832 | tf_op jit(solution)/shard_map/ppermute | solution.py:29
  135.8 27.6 %collective-permute-start.37 = (bf16[2,2,64,384]{3,2,1,0:T(8,128)(2,1)S(1)}, bf16[2,2,64,384]{3,2,1,0:T(8,128)(2,1)S(1)}, u32[]{:S(2)}, u32[]{:S(2)}) collective-permute-start(bf16[2,2,64,384]{3,2,1,0:T(8,128)(2,1)S(1)} %stack_near.1.mine), channel_id=1, source_target_pairs={{0,128},{16,144},{32,160},{48,176},{64,192},{80,208},{96,224},{112... | collective-permute-start | bytes 589832 | tf_op jit(solution)/shard_map/ppermute | solution.py:37
  139.0 29.0 %collective-permute-start.30 = (bf16[384,512]{1,0:T(8,128)(2,1)S(1)}, bf16[384,512]{1,0:T(8,128)(2,1)S(1)}, u32[]{:S(2)}, u32[]{:S(2)}) collective-permute-start(bf16[384,512]{1,0:T(8,128)(2,1)S(1)} %get-tuple-element.143), channel_id=1, source_target_pairs={{0,12},{1,13},{2,14},{3,15},{4,0},{5,1},{6,2},{7,3},{8,4},{9,5},{1... | collective-permute-start | bytes 1179656 | tf_op jit(solution)/shard_map/ppermute | solution.py:29
  140.3 27.8 %collective-permute-start.29 = (bf16[384,512]{1,0:T(8,128)(2,1)S(1)}, bf16[384,512]{1,0:T(8,128)(2,1)S(1)}, u32[]{:S(2)}, u32[]{:S(2)}) collective-permute-start(bf16[384,512]{1,0:T(8,128)(2,1)S(1)} %get-tuple-element.142), channel_id=1, source_target_pairs={{0,4},{1,5},{2,6},{3,7},{4,8},{5,9},{6,10},{7,11},{8,12},{9,13},{1... | collective-permute-start | bytes 1179656 | tf_op jit(solution)/shard_map/ppermute | solution.py:29
  159.7 16.6 %collective-permute-start.26 = (bf16[384,512]{1,0:T(8,128)(2,1)S(1)}, bf16[384,512]{1,0:T(8,128)(2,1)S(1)}, u32[]{:S(2)}, u32[]{:S(2)}) collective-permute-start(bf16[384,512]{1,0:T(8,128)(2,1)S(1)} %get-tuple-element.130), channel_id=1, source_target_pairs={{0,4},{1,5},{2,6},{3,7},{4,8},{5,9},{6,10},{7,11},{8,12},{9,13},{1... | collective-permute-start | bytes 1179656 | tf_op jit(solution)/shard_map/ppermute | solution.py:29
  159.8 16.7 %collective-permute-start.27 = (bf16[384,512]{1,0:T(8,128)(2,1)S(1)}, bf16[384,512]{1,0:T(8,128)(2,1)S(1)}, u32[]{:S(2)}, u32[]{:S(2)}) collective-permute-start(bf16[384,512]{1,0:T(8,128)(2,1)S(1)} %get-tuple-element.131), channel_id=1, source_target_pairs={{0,12},{1,13},{2,14},{3,15},{4,0},{5,1},{6,2},{7,3},{8,4},{9,5},{1... | collective-permute-start | bytes 1179656 | tf_op jit(solution)/shard_map/ppermute | solution.py:29
  163.4 15.2 %collective-permute-start.38 = (bf16[4,2,64,384]{3,2,1,0:T(8,128)(2,1)S(1)}, bf16[4,2,64,384]{3,2,1,0:T(8,128)(2,1)S(1)}, u32[]{:S(2)}, u32[]{:S(2)}) collective-permute-start(bf16[4,2,64,384]{3,2,1,0:T(8,128)(2,1)S(1)} %stack_far.1.mine), channel_id=1, source_target_pairs={{0,16},{16,0},{32,48},{48,32},{64,80},{80,64},{96,112},{112,96},{1... | collective-permute-start | bytes 1179656 | tf_op jit(solution)/shard_map/ppermute | solution.py:41
